TPU v7x, 256 devices: a whole 4x4x8 slice. The times are simulated.
256 devices in a mesh: wave: 32 (over x, z), field: 8 (over y, core).
Axes of the slice: x: 4, y: 4, z: 8, core: 2. Of those that a mesh axis runs over, the one named last changes fastest.
Arguments:
- spectral: bfloat16 [512, 2, 2, 48, 1025], P(('wave', 'field')), may hold values from -6 to 6
- legendre: bfloat16 [512, 1025, 1280], P(('wave', 'field')), may hold values from -0.1875 to 0.1875
- slot_pairs: int32 [512], replicated, may hold values from 0 to 511, each once
Outputs:
- grid_values: bfloat16 [48, 2560, 5120], P(None, 'wave', 'field')
Inputs may be any that keep to these rules, and one draw needn't show every extreme that they name: `slot_pairs`: every pair 0 to 511 stands in exactly one slot.
All inputs are finite; a program needn't handle non-finite values.
Results may differ from a plain program's by a relative error of at most 0.0058.
Values may be sent and summed in bfloat16 or wider, within the bound.
A program may use at most 128 MiB of HBM per device.

v0:
```python
import math

import jax
import jax.numpy as jnp
from jax import lax
from jax.sharding import PartitionSpec as P

M = 1024
NLON = 5120


def row_masks(pair_ids, degree_top):
    row_index = jnp.arange(degree_top + 1, dtype=jnp.int32)
    boundary = (degree_top - pair_ids)[:, None]
    first_half = row_index[None, :] < boundary
    distance = jnp.where(first_half, row_index[None, :], row_index[None, :] - boundary)
    even_rows = distance % 2 == 0
    owners = jnp.stack([first_half, jnp.logical_not(first_half)], axis=1)
    parity = jnp.stack([even_rows, jnp.logical_not(even_rows)], axis=1)
    return jnp.logical_and(parity[:, :, None, :], owners[:, None, :, :])


def masked_terms(spectral, pair_ids, degree_top):
    selector = row_masks(pair_ids, degree_top)
    zero_value = jnp.zeros((), jnp.bfloat16)
    return jnp.where(selector[:, :, :, None, None, :], spectral[:, None], zero_value)


def slot_order(position, wave_count, groups, per_device):
    group_of = position // (wave_count * per_device)
    wave_of = position // per_device % wave_count
    within = position % per_device
    return (wave_of * groups + group_of) * per_device + within


def column_basis(columns, slot_pairs, wave_count, groups, per_device, longitudes):
    position = columns // 4
    member = columns // 2 % 2
    part_index = columns % 2
    pair_ids = slot_pairs[slot_order(position, wave_count, groups, per_device)]
    numbers = jnp.where(member == 0, pair_ids, M - 1 - pair_ids)
    phase_index = numbers[:, None] * longitudes[None, :] % NLON
    angles = phase_index.astype(jnp.float32) * (2.0 * math.pi / NLON)
    weight = jnp.where(numbers == 0, 1.0 / math.sqrt(2.0 * M), 2.0 / math.sqrt(2.0 * M)).astype(
        jnp.float32
    )
    cosine = weight[:, None] * jnp.cos(angles)
    sine_part = -weight[:, None] * jnp.sin(angles)
    return jnp.where(part_index[:, None] == 0, cosine, sine_part).astype(jnp.bfloat16)


def shards(spectral, legendre, slot_pairs):
    wave_count = lax.axis_size("wave")
    groups = lax.axis_size("field")
    per_device = spectral.shape[0]
    field_levels = spectral.shape[3]
    start_slot = lax.axis_index(("wave", "field")) * per_device
    own_pairs = lax.dynamic_slice_in_dim(slot_pairs, start_slot, per_device)
    masked = masked_terms(spectral, own_pairs, M)
    masked = masked.reshape(per_device, 2, 4, field_levels, M + 1)
    legendre_sums = jnp.einsum(
        "kpxfr,krj->jpfkx", masked, legendre, preferred_element_type=jnp.float32
    )
    northern = legendre_sums[:, 0] + legendre_sums[:, 1]
    southern = jnp.flip(legendre_sums[:, 0] - legendre_sums[:, 1], axis=0)
    fourier = jnp.concatenate([northern, southern], axis=0).astype(jnp.bfloat16)
    banded = lax.all_to_all(fourier, "wave", split_axis=0, concat_axis=2, tiled=True)
    band_rows = banded.shape[0]
    banded = banded.reshape(band_rows, field_levels, banded.shape[2] * 4)
    lon_local = NLON // groups
    longitudes = lax.axis_index("field") * lon_local + jnp.arange(lon_local, dtype=jnp.int32)
    shard_piece = lax.all_gather(banded, "field", axis=2, tiled=True)
    columns = jnp.arange(shard_piece.shape[2], dtype=jnp.int32)
    basis_rows = column_basis(columns, slot_pairs, wave_count, groups, per_device, longitudes)
    summed = jnp.einsum("bfa,al->fbl", shard_piece, basis_rows, preferred_element_type=jnp.float32)
    return summed.astype(jnp.bfloat16)


def solution(mesh):
    in_specs = (P(("wave", "field"), None, None, None, None), P(("wave", "field"), None, None), P())
    out_specs = P(None, "wave", "field")
    return jax.shard_map(shards, mesh=mesh, in_specs=in_specs, out_specs=out_specs, check_vma=False)
```

profile of v0, /device:TPU:1, one launch (start us, length us, event | category | flops | bytes accessed | tf_op | source)
XLA Modules:
  0.0 229.2 jit_solution(10151582751518168421)
XLA Ops:
  6.5 0.0 all-gather.2.cloned.1.call-start
  6.5 0.8 dynamic-slice_subtract_fusion
  7.3 0.1 fusion.26
  7.4 0.1 pad_add_fusion
  7.6 5.5 %fusion.7 = f32[1280,2,48,2,4]{0,2,4,1,3:T(8,128)S(1)} fusion(bf16[2,1025,1280,1,1]{2,0,1,4,3:T(2,128)(2,1)} %bitcast.43, pred[2,2,4,1025]{3,2,1,0:T(4,128)(4,1)S(1)} %broadcast_in_dim.66, bf16[2,4,48,1025]{3,2,1,0:T(8,128)(2,1)} %bitcast.44), kind=kOutput, calls=%fused_computation.12 | convolution fusion | flops 2016019200 | bytes 9983760 | tf_op jit(solution)/shard_map/kpxfr,krj->jpfkx/dot_general | solution.py:61
  13.1 0.2 fusion.23
  13.3 0.2 subtract_bitcast_fusion
  13.5 3.9 %rev.4 = bf16[1280,48,2,4]{0,1,3,2:T(8,128)(2,1)} reverse(bf16[1280,48,2,4]{0,1,3,2:T(8,128)(2,1)S(1)} %subtract_bitcast_fusion), dimensions={0} | reverse | bytes 1966080 | tf_op jit(solution)/shard_map/jit(_flip)/rev | solution.py:65
  17.4 1.4 pad_maximum_fusion
  18.8 5.3 %copy.19 = bf16[2560,48,2,4]{1,3,2,0:T(4,128)(2,1)} copy(bf16[2560,48,2,4]{0,1,3,2:T(8,128)(2,1)S(1)} %pad_maximum_fusion) | data formatting | bytes 3932160 | tf_op jit(solution)/shard_map/concatenate | solution.py:66
  24.1 11.5 %reshape.443 = bf16[32,2,15360]{2,1,0:T(2,128)(2,1)S(1)} reshape(bf16[2560,2,4,48]{3,2,1,0:T(4,128)(2,1)} %bitcast.39) | data formatting | bytes 3932160
  35.5 56.2 %all_to_all.15 = bf16[32,2,15360]{2,1,0:T(2,128)(2,1)} all-to-all(bf16[32,2,15360]{2,1,0:T(2,128)(2,1)S(1)} %reshape.443), channel_id=1, replica_groups=mesh['wave'=32,'field'=8] {'wave'}, dimensions={0} | all-to-all | bytes 3932160 | tf_op jit(solution)/shard_map/all_to_all | solution.py:67
  91.7 13.4 %reshape.444 = bf16[2560,2,4,48]{3,2,1,0:T(4,128)(2,1)} reshape(bf16[32,2,15360]{2,1,0:T(2,128)(2,1)} %all_to_all.15) | data formatting | bytes 3932160
  105.1 7.2 %copy.20 = bf16[32,80,48,2,4]{1,2,4,3,0:T(8,128)(2,1)S(1)} copy(bf16[32,80,48,2,4]{2,4,3,1,0:T(4,128)(2,1)} %bitcast.40) | data formatting | bytes 3932160 | tf_op jit(solution)/shard_map/all_to_all | solution.py:67
  112.3 0.0 copy-start
  112.4 3.0 %copy.21 = bf16[80,48,256]{2,0,1:T(8,128)(2,1)} copy(bf16[80,48,256]{0,1,2:T(8,128)(2,1)S(1)} %bitcast.41) | data formatting | bytes 3932160 | tf_op jit(solution)/shard_map/reshape | solution.py:69
  115.3 0.0 all-gather.2.cloned.1.call-update
  115.3 0.1 compare_select_fusion
  115.4 0.0 copy-done
  115.4 13.2 %gather_fusion = s32[2048]{0:T(1024)S(1)} fusion(s32[512]{0:T(512)S(1)} %copy-done, s32[2048]{0:T(1024)S(1)} %broadcast_clamp_fusion), kind=kCustom, calls=%fused_computation | custom fusion | bytes 24576 | tf_op jit(solution)/shard_map/gather | solution.py:40
  128.7 24.0 %fusion.51 = bf16[2048,640,1]{1,0,2:T(8,128)(2,1)S(1)} fusion(f32[2048]{0:T(1024)S(1)} %fusion.44, s32[640]{0:T(1024)S(1)} %iota_add_fusion, s32[2048]{0:T(1024)S(1)} %get-tuple-element.6, f32[2048]{0:T(1024)S(1)} %get-tuple-element.5, pred[2048]{0:T(1024)(128)(4,1)S(1)} %fusion.29), kind=kLoop, calls=%fused_computation.13.clone.clone.1 | loop fusion | flops 17039360 | bytes 2650624 | tf_op jit(solution)/shard_map/bfa,al->fbl/dot_general | solution.py:75
  152.7 52.4 %all-gather.2.cloned.1.call-done = bf16[80,48,2048]{2,0,1:T(8,128)(2,1)} async-done(((bf16[80,48,256]{2,0,1:T(8,128)(2,1)}), bf16[80,48,2048]{2,0,1:T(8,128)(2,1)}) %all-gather.2.cloned.1.call-update) | async-done | bytes 15728656 | tf_op jit(solution)/shard_map/all_gather | solution.py:72
  205.1 17.2 %convert_bitcast_fusion = bf16[48,80,640]{2,1,0:T(8,128)(2,1)} fusion(bf16[80,48,2048]{2,0,1:T(8,128)(2,1)} %all-gather.2.cloned.1.call-done, bf16[2048,640,1]{1,0,2:T(8,128)(2,1)S(1)} %fusion.51), kind=kOutput, calls=%fused_computation.11 | convolution fusion | flops 10068787200 | bytes 23265280 | tf_op jit(solution)/shard_map/bfa,al->fbl/dot_general | solution.py:75
  (8 shorter events, 0.2 us)
Async XLA Ops:
  6.5 198.6 %all-gather.2.cloned.1.call-start = ((), (), s32[]{:S(2)}) async-start(), calls=%async_computation.1 | async-start | bytes 17694720 | tf_op jit(solution)/shard_map/all_gather | solution.py:72
  112.3 3.1 %copy-start = (s32[512]{0:T(512)S(1)}, s32[512]{0:T(512)}, u32[]{:S(2)}) copy-start(s32[512]{0:T(512)} %param.5) | copy-start | bytes 6148
Sparse Core Ops, SparseCore 0:
  115.5 89.5 all-gather.1
where the time goes:
time: 230 us; the launch traced here: 229 us
  local copies, waits for them, and re-layouts  57.5 us (25%)
  blocking collectives  56.2 us (24%)
  waiting for transfers between devices  52.4 us (23%)
  other arithmetic  26.8 us (12%)
  matrix products  22.7 us (10%)
  between operations  13.5 us (6%)
    all_to_all x1, blocking collectives, shards(): lax.all_to_all(fourier, 'wave', split_axis=0, concat_axis=2, tiled=True)  56.2 us
    all_gather x1, waiting for transfers between devices, shards(): shard_piece = lax.all_gather(banded, 'field', axis=2, tiled=True)  52.4 us
    unnamed x4, local copies, waits for them, and re-layouts  24.9 us
    dot_general x1, other arithmetic, shards(): jnp.einsum('bfa,al->fbl', shard_piece, basis_rows, preferred_element_type...  24 us
    dot_general x1, matrix products, shards(): jnp.einsum('bfa,al->fbl', shard_piece, basis_rows, preferred_element_type...  17.2 us
    gather x1, local copies, waits for them, and re-layouts, column_basis(): pair_ids = slot_pairs[slot_order(position, wave_count, groups, per_device)]  13.2 us
    all_to_all x1, local copies, waits for them, and re-layouts, shards(): lax.all_to_all(fourier, 'wave', split_axis=0, concat_axis=2, tiled=True)  7.19 us
    dot_general x1, matrix products, shards(): jnp.einsum('kpxfr,krj->jpfkx', masked, legendre, preferred_element_type=j...  5.5 us
  transfers between devices with their start and end apart: 1, of which 1 were waited for; matrix products, arithmetic and copies ran while one was open for 16% of the time, Pallas kernels for 0%

commit v1 on v0

v1 whole, which is shorter than its diff:
```python
import functools
import math

import jax
import jax.numpy as jnp
from jax import lax
from jax.experimental import pallas as pl
from jax.experimental.pallas import tpu as pltpu
from jax.sharding import PartitionSpec as P

M = 1024
NLON = 5120
NORTH = 1280
FLEV = 48
XS, ZS, YS = 4, 8, 4
WAVES = XS * ZS
FIELDS = 2 * YS
BAND = 80
LONS = 640
PIECE = 16
PIECES = BAND // PIECE
LANES = 8 * FLEV
DEPTH = 8 * WAVES
MESH = pl.DeviceIdType.MESH
F32 = jnp.float32
BF16 = jnp.bfloat16


def iota(shape, dim):
    return lax.broadcasted_iota(jnp.int32, shape, dim)


def one_hot(condition):
    return jnp.where(condition, 1.0, 0.0).astype(BF16)


def legendre_kernel(pairs_ref, spectral_ref, legendre_ref, send_ref, sums):
    slot = pl.program_id(0)
    pair = pairs_ref[slot]
    rows = M + 1
    boundary = M - pair
    row = iota((2 * FLEV, rows), 1)
    in_first = row < boundary
    distance = jnp.where(in_first, row, row - boundary)
    sign = jnp.where(distance % 2 == 0, 1.0, -1.0)
    first = spectral_ref[0, : 2 * FLEV, :].astype(F32)
    second = spectral_ref[0, 2 * FLEV :, :].astype(F32)
    first = jnp.where(in_first, first, 0.0)
    second = jnp.where(in_first, 0.0, second)
    terms = jnp.concatenate([first, second, first * sign, second * sign], axis=0).astype(BF16)
    sums[slot] = jnp.dot(terms, legendre_ref[0], preferred_element_type=F32).astype(BF16)

    @pl.when(slot == 1)
    def _():
        half = 4 * FLEV
        target = iota((LANES, LANES), 0)
        source = target % 8 // 4 * half + target % 4 * FLEV + target // 8
        order = one_hot(iota((LANES, LANES), 1) == source)
        lat = iota((BAND, 256), 0)
        col = iota((BAND, 256), 1)
        for south in range(2):
            stacked = jnp.concatenate(
                [sums[k, south * half : (south + 1) * half, :] for k in range(2)], axis=0
            )
            ordered = jnp.dot(order, stacked, preferred_element_type=F32).astype(BF16)
            for band in range(NORTH // BAND):
                start = min(band * BAND // 128 * 128, NORTH - 256)
                offset = band * BAND - start
                pick = one_hot(col == (offset + BAND - 1 - lat if south else offset + lat))
                chunk = lax.dot_general(
                    pick,
                    ordered[:, start : start + 256],
                    (((1,), (1,)), ((), ())),
                    preferred_element_type=F32,
                )
                send_ref[WAVES - 1 - band if south else band] = chunk.astype(BF16)


def legendre_stage(own_pairs, spectral, legendre):
    return pl.pallas_call(
        legendre_kernel,
        grid=(2,),
        out_shape=jax.ShapeDtypeStruct((WAVES, BAND, LANES), BF16),
        in_specs=[
            pl.BlockSpec(memory_space=pltpu.SMEM),
            pl.BlockSpec((1, 4 * FLEV, M + 1), lambda k: (k, 0, 0)),
            pl.BlockSpec((1, M + 1, NORTH), lambda k: (k, 0, 0)),
        ],
        out_specs=pl.BlockSpec((WAVES, BAND, LANES), lambda k: (0, 0, 0)),
        scratch_shapes=[pltpu.VMEM((2, 8 * FLEV, NORTH), BF16)],
        compiler_params=pltpu.CompilerParams(vmem_limit_bytes=40 << 20),
        name="legendre",
    )(own_pairs, spectral, legendre)


COS = [(-1.0) ** k * (2.0 * math.pi) ** (2 * k) / math.factorial(2 * k) for k in range(12)]


def grid_kernel(
    send_ref, number_ref, out_ref,
    landed, whole, basis, swap_outer, swap_inner, result,
    a2a_send, a2a_recv, y_send, y_recv, fwd_send, fwd_recv, core_send, core_recv, out_sem,
):
    wave = lax.axis_index("wave")
    field = lax.axis_index("field")
    x, z = wave // ZS, wave % ZS
    y, core = field // 2, field % 2
    up = lax.rem(y + 1, YS) * 2 + core
    down = lax.rem(y + YS - 1, YS) * 2 + core
    across = lax.rem(y + 2, YS) * 2 + core
    other = 1 - core
    mate = y * 2 + other

    def peer_of(i):
        return lax.rem(x + i // ZS, XS) * ZS + lax.rem(z + i % ZS, ZS)

    barrier = pltpu.get_barrier_semaphore()
    for there in (up, down, mate):
        pl.semaphore_signal(barrier, inc=1, device_id=(wave, there), device_id_type=MESH)

    def greet(i, carry):
        pl.semaphore_signal(barrier, inc=1, device_id=(peer_of(i), field), device_id_type=MESH)
        return carry

    lax.fori_loop(1, WAVES, greet, 0)
    pl.semaphore_wait(barrier, WAVES + 2)

    def scatter(p):
        def one(i, carry):
            peer = peer_of(i)
            pltpu.make_async_remote_copy(
                src_ref=send_ref.at[peer, pl.ds(p * PIECE, PIECE), :],
                dst_ref=landed.at[p, wave],
                send_sem=a2a_send.at[p],
                recv_sem=a2a_recv.at[p],
                device_id=(peer, field),
                device_id_type=MESH,
            ).start()
            return carry

        lax.fori_loop(1, WAVES, one, 0)
        landed[p, wave] = send_ref[wave, p * PIECE : (p + 1) * PIECE, :]

    def wait_all(p, sem):
        block = landed.at[p, pl.ds(0, WAVES - 1)]
        pltpu.make_async_copy(block, block, sem.at[p]).wait()

    half = FLEV // 2

    def remote(p, source, part, send, recv, slot, there):
        lo, size = ((0, FLEV), (0, half), (half, half))[part]
        block = whole.at[p, source, pl.ds(lo, size)]
        return pltpu.make_async_remote_copy(
            src_ref=block, dst_ref=block, send_sem=send.at[p, slot], recv_sem=recv.at[p, slot],
            device_id=(wave, there), device_id_type=MESH,
        )

    def to_up(p):
        return remote(p, field, 0, y_send, y_recv, 0, up)

    def to_down(p):
        return remote(p, field, 0, y_send, y_recv, 1, down)

    def fwd_up(p):
        return remote(p, down, 1, fwd_send, fwd_recv, 0, up)

    def fwd_down(p):
        return remote(p, up, 2, fwd_send, fwd_recv, 1, down)

    def to_mate(p, k):
        source, part = ((field, 0), (down, 0), (up, 0), (across, 1), (across, 2))[k]
        return remote(p, source, part, core_send, core_recv, k, mate)

    def from_mate(p, k):
        yy = lambda s: s // 2 * 2 + other
        source, part = ((yy(field), 0), (yy(down), 0), (yy(up), 0), (yy(across), 1), (yy(across), 2))[k]
        return remote(p, source, part, core_send, core_recv, k, mate)

    def from_down(p):
        return remote(p, down, 0, y_send, y_recv, 0, down)

    def from_up(p):
        return remote(p, up, 0, y_send, y_recv, 1, up)

    def half_from_down(p):
        return remote(p, across, 1, fwd_send, fwd_recv, 0, down)

    def half_from_up(p):
        return remote(p, across, 2, fwd_send, fwd_recv, 1, up)

    def gather(p):
        wait_all(p, a2a_recv)
        got = landed[p].reshape(2, 4, 4, PIECE, LANES)
        groups = LANES // 128
        rows = groups * 8 * PIECE
        lhs = jnp.concatenate(
            [
                jnp.concatenate(
                    [
                        got[:, s1, :, :, 128 * g : 128 * (g + 1)].reshape(8 * PIECE, 128)
                        for g in range(groups)
                    ],
                    axis=0,
                )
                for s1 in range(4)
            ],
            axis=1,
        )
        mixed = jnp.dot(lhs, swap_outer[...], preferred_element_type=F32).astype(BF16)
        mixed = mixed.reshape(groups * 2, 4, PIECE, 512)
        lhs = jnp.concatenate(
            [
                jnp.concatenate(
                    [
                        mixed[:, s0, :, 128 * f1 : 128 * (f1 + 1)].reshape(groups * 2 * PIECE, 128)
                        for f1 in range(4)
                    ],
                    axis=0,
                )
                for s0 in range(4)
            ],
            axis=1,
        )
        done = jnp.dot(lhs, swap_inner[...], preferred_element_type=F32).astype(BF16)
        done = done.reshape(4, groups, 2, PIECE, 512)
        for f1 in range(4):
            for g in range(groups):
                for f0 in range(4):
                    for s in range(2):
                        whole[p, field, g * 16 + f1 * 4 + f0, :, 128 * s : 128 * (s + 1)] = done[
                            f1, g, s, :, 128 * f0 : 128 * (f0 + 1)
                        ]
        to_up(p).start()
        to_down(p).start()
        to_mate(p, 0).start()

    def relay(p):
        from_down(p).wait_recv()
        fwd_up(p).start()
        to_mate(p, 1).start()
        from_up(p).wait_recv()
        fwd_down(p).start()
        to_mate(p, 2).start()

    def finish(p):
        half_from_down(p).wait_recv()
        to_mate(p, 3).start()
        half_from_up(p).wait_recv()
        to_mate(p, 4).start()

    def out_copy(p, slot):
        return pltpu.make_async_copy(
            result.at[slot], out_ref.at[:, pl.ds(p * PIECE, PIECE), :], out_sem.at[slot]
        )

    def synthesize(p):
        for k in range(5):
            from_mate(p, k).wait_recv()
        slot = p % 2
        if p >= 2:
            out_copy(p - 2, slot).wait()
        levels = 12

        def block(i, carry):
            at = pl.ds(pl.multiple_of(i * levels, levels), levels)
            lhs = jnp.concatenate(
                [whole[p, s, at].reshape(levels * PIECE, DEPTH) for s in range(FIELDS)], axis=1
            )
            summed = jnp.dot(lhs, basis[...], preferred_element_type=F32)
            result[slot, at] = summed.astype(BF16).reshape(levels, PIECE, LONS)
            return carry

        lax.fori_loop(0, FLEV // levels, block, 0)
        out_copy(p, slot).start()

    scatter(0)
    scatter(1)

    a, b = iota((512, 512), 0), iota((512, 512), 1)
    swap_outer[...] = one_hot(b == a // 32 % 4 * 128 + a // 128 * 32 + a % 32)
    swap_inner[...] = one_hot(b == a // 8 % 4 * 128 + a // 32 % 4 * 32 + a // 128 * 8 + a % 8)

    def basis_block(i, carry):
        size = 128
        at = pl.ds(pl.multiple_of(i * size, size), size)
        number = number_ref[at, :]
        part = (iota((size, 1), 0) % 2).astype(F32)
        weight = jnp.where(number == 0.0, 1.0 / math.sqrt(2.0 * M), 2.0 / math.sqrt(2.0 * M))
        longitude = (field * LONS + iota((size, LONS), 1)).astype(F32)
        phase = number * longitude + part * (NLON // 4)
        phase = phase - NLON * jnp.floor(phase * (1.0 / NLON) + 0.5)
        turn = phase * (1.0 / NLON)
        square = turn * turn
        value = COS[-1]
        for c in COS[-2::-1]:
            value = value * square + c
        basis[at, :] = (weight * value).astype(BF16)
        return carry

    lax.fori_loop(0, DEPTH * FIELDS // 128, basis_block, 0)

    for t in range(PIECES + 3):
        if t < PIECES:
            gather(t)
            if t + 2 < PIECES:
                scatter(t + 2)
        if 0 <= t - 1 < PIECES:
            relay(t - 1)
        if 0 <= t - 2 < PIECES:
            finish(t - 2)
        if 0 <= t - 3 < PIECES:
            synthesize(t - 3)

    for p in range(PIECES):
        wait_all(p, a2a_send)
        to_up(p).wait_send()
        to_down(p).wait_send()
        fwd_up(p).wait_send()
        fwd_down(p).wait_send()
        for k in range(5):
            to_mate(p, k).wait_send()
    out_copy(PIECES - 2, (PIECES - 2) % 2).wait()
    out_copy(PIECES - 1, (PIECES - 1) % 2).wait()


def grid_stage(send, numbers):
    dma = pltpu.SemaphoreType.DMA
    return pl.pallas_call(
        grid_kernel,
        out_shape=jax.ShapeDtypeStruct((FLEV, BAND, LONS), BF16),
        in_specs=[pl.BlockSpec(memory_space=pltpu.VMEM)] * 2,
        out_specs=pl.BlockSpec(memory_space=pl.ANY),
        scratch_shapes=[
            pltpu.VMEM((PIECES, WAVES, PIECE, LANES), BF16),
            pltpu.VMEM((PIECES, FIELDS, FLEV, PIECE, DEPTH), BF16),
            pltpu.VMEM((DEPTH * FIELDS, LONS), BF16),
            pltpu.VMEM((512, 512), BF16),
            pltpu.VMEM((512, 512), BF16),
            pltpu.VMEM((2, FLEV, PIECE, LONS), BF16),
            dma((PIECES,)), dma((PIECES,)),
            dma((PIECES, 2)), dma((PIECES, 2)),
            dma((PIECES, 2)), dma((PIECES, 2)),
            dma((PIECES, 5)), dma((PIECES, 5)),
            dma((2,)),
        ],
        compiler_params=pltpu.CompilerParams(
            collective_id=0, has_side_effects=True, vmem_limit_bytes=56 << 20
        ),
        name="grid",
    )(send, numbers)


def shards(spectral, legendre, slot_pairs):
    per_device = spectral.shape[0]
    start_slot = lax.axis_index(("wave", "field")) * per_device
    own_pairs = lax.dynamic_slice_in_dim(slot_pairs, start_slot, per_device)
    send = legendre_stage(own_pairs, spectral.reshape(per_device, 4 * FLEV, M + 1), legendre)
    pairs = slot_pairs.reshape(WAVES, FIELDS, per_device).transpose(1, 0, 2).reshape(-1)
    numbers = jnp.stack([pairs, M - 1 - pairs], axis=1).reshape(-1, 1)
    numbers = jnp.repeat(numbers, 2, axis=0)
    return grid_stage(send, numbers.astype(F32))


def solution(mesh):
    in_specs = (P(("wave", "field"), None, None, None, None), P(("wave", "field"), None, None), P())
    out_specs = P(None, "wave", "field")
    return jax.shard_map(shards, mesh=mesh, in_specs=in_specs, out_specs=out_specs, check_vma=False)
```

time: 230 us -> 117 us (0.51)
  Pallas kernels: 0 us -> 103 us
  blocking collectives: 56.2 us -> 0 us
  waiting for transfers between devices: 52.4 us -> 0 us
  local copies, waits for them, and re-layouts: 57.5 us -> 13 us
  other arithmetic: 26.8 us -> 0.02 us
  matrix products: 22.7 us -> 0 us
  between operations: 13.5 us -> 0.09 us
    pallas_call x0 -> x2, Pallas kernels: none -> 103 us  [the longest x1 96.9 us: grid_stage(): pl.pallas_call(grid_kernel, out_shape=jax.ShapeDtypeStruct((FLEV, BAND, L...]
    all_to_all x1 -> x0, blocking collectives: 56.2 us -> none  [shards(): lax.all_to_all(fourier, 'wave', split_axis=0, concat_axis=2, tiled=True)]
    all_gather x1 -> x0, waiting for transfers between devices: 52.4 us -> none  [shards(): shard_piece = lax.all_gather(banded, 'field', axis=2, tiled=True)]
    dot_general x1 -> x0, other arithmetic: 24 us -> none  [shards(): jnp.einsum('bfa,al->fbl', shard_piece, basis_rows, preferred_element_type...]
    dot_general x2 -> x0, matrix products: 22.7 us -> none  [the longest x1 17.2 us: shards(): jnp.einsum('bfa,al->fbl', shard_piece, basis_rows, preferred_element_type...]
    unnamed x4 -> x6, local copies, waits for them, and re-layouts: 24.9 us -> 9.56 us
    gather x1 -> x0, local copies, waits for them, and re-layouts: 13.2 us -> none  [column_basis(): pair_ids = slot_pairs[slot_order(position, wave_count, groups, per_device)]]
    all_to_all x1 -> x0, local copies, waits for them, and re-layouts: 7.19 us -> none  [shards(): lax.all_to_all(fourier, 'wave', split_axis=0, concat_axis=2, tiled=True)]
  transfers between devices with their start and end apart: 1 -> 0, of which waited for: 1 -> 0; matrix products, arithmetic and copies ran while one was open for 16% -> 0% of each run, Pallas kernels for 0% -> 0%
where the time goes in v1:
time: 117 us; the launch traced here: 116 us
  Pallas kernels  103 us (88%)
  local copies, waits for them, and re-layouts  13 us (11%)
    pallas_call x1, Pallas kernels, grid_stage(): pl.pallas_call(grid_kernel, out_shape=jax.ShapeDtypeStruct((FLEV, BAND, L...  96.9 us
    unnamed x6, local copies, waits for them, and re-layouts  9.56 us
    pallas_call x1, Pallas kernels, legendre_stage(): pl.pallas_call(legendre_kernel, grid=(2,), out_shape=jax.ShapeDtypeStruct...  6.45 us

profile of v1, /device:TPU:1, one launch (start us, length us, event | category | flops | bytes accessed | tf_op | source)
XLA Modules:
  0.0 116.4 jit_solution(17694511433614405146)
XLA Ops:
  0.0 0.8 dynamic_slice.3.pairs_ref
  0.8 0.8 reshape.39
  1.6 0.1 stack_reshape.3
  1.8 0.1 copy.7
  1.9 0.2 convert_element_type.8
  2.1 0.2 broadcast_in_dim.3
  2.3 1.2 %convert_element_type.10.number_ref = f32[2048,1]{1,0:T(8,128)} reshape(f32[1024,2]{1,0:T(8,128)S(1)} %broadcast_in_dim.3) | data formatting | bytes 16384 | tf_op jit(solution)/shard_map/convert_element_type | solution.py:361
  3.5 0.0 copy-start.1
  3.5 3.2 %copy.5.legendre_ref = bf16[2,1025,1280]{2,1,0:T(8,128)(2,1)S(1)} copy(bf16[2,1025,1280]{2,0,1:T(2,128)(2,1)} %param.4) | data formatting | bytes 10496000 | tf_op args[1]
  6.8 0.0 copy-done.1
  6.8 6.5 %legendre.1.send_ref = bf16[32,80,384]{2,1,0:T(8,128)(2,1)S(1)} custom-call(s32[2]{0:T(128)S(1)} %dynamic_slice.3.pairs_ref, bf16[2,192,1025]{2,1,0:T(8,128)(2,1)S(1)} %bitcast.2, bf16[2,1025,1280]{2,1,0:T(8,128)(2,1)S(1)} %copy.5.legendre_ref), custom_call_target="tpu_custom_call" | custom-call | tf_op jit(solution)/shard_map/legendre/pallas_call | solution.py:80
  13.2 0.0 copy-start
  13.2 1.3 %copy-done = bf16[32,80,384]{2,1,0:T(8,128)(2,1)} copy-done((bf16[32,80,384]{2,1,0:T(8,128)(2,1)}, bf16[32,80,384]{2,1,0:T(8,128)(2,1)S(1)}, u32[]{:S(2)}) %copy-start) | copy-done | bytes 1966104
  14.5 96.9 %grid.1 = bf16[48,80,640]{2,1,0:T(8,128)(2,1)} custom-call(bf16[32,80,384]{2,1,0:T(8,128)(2,1)} %copy-done, f32[2048,1]{1,0:T(8,128)} %convert_element_type.10.number_ref), custom_call_target="tpu_custom_call" | custom-call | tf_op jit(solution)/shard_map/grid/pallas_call | solution.py:328
  111.4 5.1 %copy.10 = bf16[48,80,640]{2,1,0:T(8,128)(2,1)} copy(bf16[48,80,640]{2,1,0:T(8,128)(2,1)} %grid.1) | data formatting | bytes 9830400
  (3 shorter events, 0.0 us)
Async XLA Ops:
  3.5 3.2 %copy-start.1 = (bf16[2,2,2,48,1025]{4,3,2,1,0:T(8,128)(2,1)S(1)}, bf16[2,2,2,48,1025]{4,3,2,1,0:T(8,128)(2,1)}, u32[]{:S(2)}) copy-start(bf16[2,2,2,48,1025]{4,3,2,1,0:T(8,128)(2,1)} %param.3) | copy-start | bytes 2361604
  13.2 1.3 %copy-start = (bf16[32,80,384]{2,1,0:T(8,128)(2,1)}, bf16[32,80,384]{2,1,0:T(8,128)(2,1)S(1)}, u32[]{:S(2)}) copy-start(bf16[32,80,384]{2,1,0:T(8,128)(2,1)S(1)} %legendre.1.send_ref) | copy-start | bytes 5898244

commit v2 on v0

v2 whole, which is shorter than its diff:
```python
import math

import jax
import jax.numpy as jnp
from jax import lax
from jax.experimental import pallas as pl
from jax.experimental.pallas import tpu as pltpu
from jax.sharding import PartitionSpec as P

M = 1024
PAIRS = 512
NLON = 5120
NORTH = 1280
FLEV = 48
XS, ZS, YS = 4, 8, 4
WAVES = XS * ZS
FIELDS = 2 * YS
BAND = 80
LONS = 640
TILE = 16
PIECES = BAND // TILE
GROUPS = FLEV // TILE
STEPS = PIECES * GROUPS
HALF = 4 * FLEV
LANES = 8 * FLEV
DEPTH = 8 * WAVES
LAG_RELAY, LAG_FINISH, LAG_GRID = 2, 3, 4
BASIS_FROM, BASIS_STEPS = 3, 4
CAUGHT_UP = 2 * (BASIS_FROM + BASIS_STEPS) - LAG_GRID
MESH = pl.DeviceIdType.MESH
F32 = jnp.float32
BF16 = jnp.bfloat16
SINE = [(-1.0) ** k * (2.0 * math.pi) ** (2 * k + 1) / math.factorial(2 * k + 1) for k in range(8)]


def iota(shape, dim):
    return lax.broadcasted_iota(jnp.int32, shape, dim)


def one_hot(condition):
    return jnp.where(condition, 1.0, 0.0).astype(BF16)


def matmul(a, b):
    return jnp.dot(a, b, preferred_element_type=F32)


def kernel(
    pairs_ref, sums_ref, out_ref,
    send, landed, whole, basis, swap_outer, swap_inner,
    a2a_send, a2a_recv, y_send, y_recv, fwd_send, fwd_recv, core_send, core_recv,
):
    wave = lax.axis_index("wave")
    field = lax.axis_index("field")
    x, z = wave // ZS, wave % ZS
    y, core = field // 2, field % 2
    up = lax.rem(y + 1, YS) * 2 + core
    down = lax.rem(y + YS - 1, YS) * 2 + core
    across = lax.rem(y + 2, YS) * 2 + core
    other = 1 - core
    mate = y * 2 + other

    def peer_of(i):
        return lax.rem(x + i // ZS, XS) * ZS + lax.rem(z + i % ZS, ZS)

    barrier = pltpu.get_barrier_semaphore()
    for there in (up, down, mate):
        pl.semaphore_signal(barrier, inc=1, device_id=(wave, there), device_id_type=MESH)

    def greet(i, carry):
        pl.semaphore_signal(barrier, inc=1, device_id=(peer_of(i), field), device_id_type=MESH)
        return carry

    lax.fori_loop(1, WAVES, greet, 0)

    def turn(g):
        a, b = iota((256, 256), 0), iota((256, 256), 1)
        for south in range(2):
            pick = one_hot(a + b == 255 if south else a == b)
            for u in range(NORTH // 256):
                start = NORTH - 256 * (u + 1) if south else 256 * u
                rows = [
                    sums_ref[k, lo : lo + TILE, start : start + 256]
                    for k in range(2)
                    for lo in range(south * HALF + g * TILE, (south + 1) * HALF, FLEV)
                ]
                turned = lax.dot_general(
                    pick,
                    jnp.concatenate(rows, axis=0),
                    (((1,), (1,)), ((), ())),
                    preferred_element_type=F32,
                )
                at = south * NORTH // TILE + u * 16
                send[at : at + 16, :, g * 128 : (g + 1) * 128] = turned.astype(BF16).reshape(
                    16, TILE, 128
                )

    def scatter(p, lane, lanes, sem):
        def one(i, carry):
            peer = peer_of(i)
            pltpu.make_async_remote_copy(
                src_ref=send.at[peer * PIECES + p, :, pl.ds(lane, lanes)],
                dst_ref=landed.at[p, wave, :, pl.ds(lane, lanes)],
                send_sem=a2a_send.at[sem],
                recv_sem=a2a_recv.at[sem],
                device_id=(peer, field),
                device_id_type=MESH,
            ).start()
            return carry

        lax.fori_loop(1, WAVES, one, 0)

    def wait_all(p, lane, lanes, sem):
        block = landed.at[p, pl.ds(0, WAVES - 1), :, pl.ds(lane, lanes)]
        pltpu.make_async_copy(block, block, sem).wait()

    def remote(t, source, part, send_sem, recv_sem, slot, there):
        lo, size = ((0, TILE), (0, TILE // 2), (TILE // 2, TILE // 2))[part]
        block = whole.at[t, source, pl.ds(lo, size)]
        return pltpu.make_async_remote_copy(
            src_ref=block, dst_ref=block,
            send_sem=send_sem.at[t, slot], recv_sem=recv_sem.at[t, slot],
            device_id=(wave, there), device_id_type=MESH,
        )

    def to_up(t, source=field):
        return remote(t, source, 0, y_send, y_recv, 0, up)

    def to_down(t, source=field):
        return remote(t, source, 0, y_send, y_recv, 1, down)

    def fwd_up(t, source=down):
        return remote(t, source, 1, fwd_send, fwd_recv, 0, up)

    def fwd_down(t, source=up):
        return remote(t, source, 2, fwd_send, fwd_recv, 1, down)

    def to_mate(t, k, flip=0):
        source, part = ((field, 0), (down, 0), (up, 0), (across, 1), (across, 2))[k]
        if flip:
            source = source // 2 * 2 + other
        return remote(t, source, part, core_send, core_recv, k, mate)

    def gather(t):
        p, g = t // GROUPS, lax.rem(t, GROUPS)

        @pl.when(p == 0)
        def _():
            wait_all(0, pl.multiple_of(g * 128, 128), 128, a2a_recv.at[g])

        @pl.when(jnp.logical_and(p > 0, g == 0))
        def _():
            wait_all(p, 0, LANES, a2a_recv.at[GROUPS - 1 + p])

        got = landed[p, :, :, pl.ds(pl.multiple_of(g * 128, 128), 128)]
        got = got.reshape(2, 4, 4, TILE, 128)
        lhs = jnp.concatenate([got[:, s1].reshape(128, 128) for s1 in range(4)], axis=1)
        mixed = matmul(lhs, swap_outer[...]).astype(BF16).reshape(2, 4, TILE, 512)
        lhs = jnp.concatenate(
            [
                jnp.concatenate(
                    [
                        mixed[:, s0, :, 128 * f1 : 128 * (f1 + 1)].reshape(2 * TILE, 128)
                        for f1 in range(4)
                    ],
                    axis=0,
                )
                for s0 in range(4)
            ],
            axis=1,
        )
        done = matmul(lhs, swap_inner[...]).astype(BF16).reshape(4, 2, TILE, 512)
        for f1 in range(4):
            for f0 in range(4):
                for s in range(2):
                    whole[t, field, f1 * 4 + f0, :, 128 * s : 128 * (s + 1)] = done[
                        f1, s, :, 128 * f0 : 128 * (f0 + 1)
                    ]
        to_up(t).start()
        to_down(t).start()
        to_mate(t, 0).start()

    def relay(t):
        to_up(t, down).wait_recv()
        fwd_up(t).start()
        to_mate(t, 1).start()
        to_down(t, up).wait_recv()
        fwd_down(t).start()
        to_mate(t, 2).start()

    def finish(t):
        fwd_up(t, across).wait_recv()
        to_mate(t, 3).start()
        fwd_down(t, across).wait_recv()
        to_mate(t, 4).start()

    def synthesize(t):
        for k in range(5):
            to_mate(t, k, 1).wait_recv()
        lhs = jnp.concatenate(
            [whole[t, s].reshape(TILE * TILE, DEPTH) for s in range(FIELDS)], axis=1
        )
        values = matmul(lhs, basis[...]).astype(BF16).reshape(TILE, TILE, LONS)
        levels = pl.ds(pl.multiple_of(lax.rem(t, GROUPS) * TILE, TILE), TILE)
        lats = pl.ds(pl.multiple_of(t // GROUPS * TILE, TILE), TILE)
        out_ref[levels, lats, :] = values

    size = 128

    def basis_block(i, carry):
        at = pl.ds(pl.multiple_of(i * size, size), size)
        r = i * size + iota((size, 1), 0)
        inside = r % DEPTH
        source = inside // 128 * 16 + inside % 16
        slot = (source * FIELDS + r // DEPTH) * 2 + inside // 64 % 2
        pairs = jnp.broadcast_to(pairs_ref[...].reshape(1, PAIRS), (size, PAIRS))
        pair = jnp.sum(
            jnp.where(iota((size, PAIRS), 1) == slot, pairs, 0).astype(F32), axis=1, keepdims=True
        )
        number = jnp.where(r // 32 % 2 == 0, pair, M - 1.0 - pair)
        part = (r // 16 % 2).astype(F32)
        weight = jnp.where(number == 0.0, 1.0 / math.sqrt(2.0 * M), 2.0 / math.sqrt(2.0 * M))
        longitude = (field * LONS + iota((size, LONS), 1)).astype(F32)
        phase = number * longitude + part * (NLON // 4)
        phase = phase - NLON * jnp.floor(phase * (1.0 / NLON) + 0.5)
        turns = 0.25 - jnp.abs(phase) * (1.0 / NLON)
        square = turns * turns
        value = SINE[-1]
        for c in SINE[-2::-1]:
            value = value * square + c
        value = value * turns
        basis[at, :] = (weight * value).astype(BF16)
        return carry

    def own(p):
        landed[p, wave] = send[wave * PIECES + p]

    def scatter_group(g):
        turn(g)
        if g == 0:
            pl.semaphore_wait(barrier, WAVES + 2)
        scatter(0, g * 128, 128, g)
        lanes = slice(g * 128, (g + 1) * 128)
        landed[0, wave, :, lanes] = send[wave * PIECES, :, lanes]

    scatter_group(0)
    scatter_group(1)

    a, b = iota((512, 512), 0), iota((512, 512), 1)
    keep = a // 16 % 8 * 16
    swap_outer[...] = one_hot(b == a // 4 % 4 * 128 + keep + a // 128 * 4 + a % 4)
    swap_inner[...] = one_hot(b == a % 4 * 128 + keep + a // 4 % 4 * 4 + a // 128)

    scatter_group(2)
    scatter(1, 0, LANES, GROUPS)
    gather(0)
    scatter(2, 0, LANES, GROUPS + 1)
    gather(1)
    relay(0)
    gather(2)
    for p in range(1, PIECES):
        own(p)

    def step(t, carry):
        p, g = t // GROUPS, lax.rem(t, GROUPS)

        @pl.when(t < STEPS + LAG_RELAY)
        def _():
            relay(t - LAG_RELAY)

        @pl.when(jnp.logical_and(g == 0, p < PIECES - 2))
        def _():
            scatter(p + 2, 0, LANES, GROUPS + 1 + p)

        @pl.when(t < STEPS)
        def _():
            gather(t)

        @pl.when(t < STEPS + LAG_FINISH)
        def _():
            finish(t - LAG_FINISH)

        @pl.when(t < BASIS_FROM + BASIS_STEPS)
        def _():
            blocks = FIELDS * DEPTH // size // BASIS_STEPS
            first = (t - BASIS_FROM) * blocks
            lax.fori_loop(first, first + blocks, basis_block, 0)

        @pl.when(jnp.logical_and(t >= BASIS_FROM + BASIS_STEPS, t < CAUGHT_UP))
        def _():
            synthesize(2 * (t - BASIS_FROM - BASIS_STEPS))
            synthesize(2 * (t - BASIS_FROM - BASIS_STEPS) + 1)

        @pl.when(t >= CAUGHT_UP)
        def _():
            synthesize(t - LAG_GRID)

        return carry

    lax.fori_loop(GROUPS, STEPS + LAG_GRID, step, 0)

    for g in range(GROUPS):
        wait_all(0, g * 128, 128, a2a_send.at[g])
    for p in range(1, PIECES):
        wait_all(p, 0, LANES, a2a_send.at[GROUPS - 1 + p])

    def drain(t, carry):
        to_up(t).wait_send()
        to_down(t).wait_send()
        fwd_up(t).wait_send()
        fwd_down(t).wait_send()
        for k in range(5):
            to_mate(t, k).wait_send()
        return carry

    lax.fori_loop(0, STEPS, drain, 0)


def hemisphere_terms(spectral, pair_ids):
    row = jnp.arange(M + 1, dtype=jnp.int32)[None, :]
    boundary = (M - pair_ids)[:, None]
    in_first = row < boundary
    odd = jnp.where(in_first, row, row - boundary) % 2 == 1
    owner = jnp.stack([in_first, jnp.logical_not(in_first)], axis=1)[:, None, :, None, None, :]
    flip = jnp.stack([jnp.zeros_like(odd), odd], axis=1)[:, :, None, None, None, :]
    terms = jnp.where(owner, spectral[:, None], jnp.zeros((), BF16))
    return jnp.where(flip, -terms, terms)


def shards(spectral, legendre, slot_pairs):
    per_device = spectral.shape[0]
    start_slot = lax.axis_index(("wave", "field")) * per_device
    own_pairs = lax.dynamic_slice_in_dim(slot_pairs, start_slot, per_device)
    terms = hemisphere_terms(spectral, own_pairs).reshape(per_device, 2 * HALF, M + 1)
    sums = jnp.einsum("kqr,krj->kqj", terms, legendre, preferred_element_type=F32).astype(BF16)
    dma = pltpu.SemaphoreType.DMA
    vmem = pltpu.VMEM
    return pl.pallas_call(
        kernel,
        out_shape=jax.ShapeDtypeStruct((FLEV, BAND, LONS), BF16),
        in_specs=[pl.BlockSpec(memory_space=pltpu.VMEM)] * 2,
        out_specs=pl.BlockSpec(memory_space=pltpu.VMEM),
        scratch_shapes=[
            vmem((WAVES * PIECES, TILE, LANES), BF16),
            vmem((PIECES, WAVES, TILE, LANES), BF16),
            vmem((STEPS, FIELDS, TILE, TILE, DEPTH), BF16),
            vmem((FIELDS * DEPTH, LONS), BF16),
            vmem((512, 512), BF16),
            vmem((512, 512), BF16),
            dma((GROUPS + PIECES - 1,)), dma((GROUPS + PIECES - 1,)),
            dma((STEPS, 2)), dma((STEPS, 2)),
            dma((STEPS, 2)), dma((STEPS, 2)),
            dma((STEPS, 5)), dma((STEPS, 5)),
        ],
        compiler_params=pltpu.CompilerParams(
            collective_id=0, has_side_effects=True, vmem_limit_bytes=40 << 20
        ),
        name="spectral_to_grid",
    )(slot_pairs, sums)


def solution(mesh):
    in_specs = (P(("wave", "field"), None, None, None, None), P(("wave", "field"), None, None), P())
    out_specs = P(None, "wave", "field")
    return jax.shard_map(shards, mesh=mesh, in_specs=in_specs, out_specs=out_specs, check_vma=False)
```

time: 230 us -> 102 us (0.44)
  Pallas kernels: 0 us -> 93.2 us
  blocking collectives: 56.2 us -> 0 us
  local copies, waits for them, and re-layouts: 57.5 us -> 3.33 us
  waiting for transfers between devices: 52.4 us -> 0 us
  other arithmetic: 26.8 us -> 2.61 us
  matrix products: 22.7 us -> 2.72 us
  between operations: 13.5 us -> 0.06 us
    pallas_call x0 -> x1, Pallas kernels: none -> 93.2 us  [shards(): pl.pallas_call(kernel, out_shape=jax.ShapeDtypeStruct((FLEV, BAND, LONS),...]
    all_to_all x1 -> x0, blocking collectives: 56.2 us -> none  [shards(): lax.all_to_all(fourier, 'wave', split_axis=0, concat_axis=2, tiled=True)]
    all_gather x1 -> x0, waiting for transfers between devices: 52.4 us -> none  [shards(): shard_piece = lax.all_gather(banded, 'field', axis=2, tiled=True)]
    dot_general x1 -> x0, other arithmetic: 24 us -> none  [shards(): jnp.einsum('bfa,al->fbl', shard_piece, basis_rows, preferred_element_type...]
    unnamed x4 -> x5, local copies, waits for them, and re-layouts: 24.9 us -> 3.3 us
    dot_general x2 -> x1, matrix products: 22.7 us -> 2.72 us  [shards(): jnp.einsum('kqr,krj->kqj', terms, legendre, preferred_element_type=F32)]
    gather x1 -> x0, local copies, waits for them, and re-layouts: 13.2 us -> none  [column_basis(): pair_ids = slot_pairs[slot_order(position, wave_count, groups, per_device)]]
    all_to_all x1 -> x0, local copies, waits for them, and re-layouts: 7.19 us -> none  [shards(): lax.all_to_all(fourier, 'wave', split_axis=0, concat_axis=2, tiled=True)]
  transfers between devices with their start and end apart: 1 -> 0, of which waited for: 1 -> 0; matrix products, arithmetic and copies ran while one was open for 16% -> 0% of each run, Pallas kernels for 0% -> 0%
where the time goes in v2:
time: 102 us
  Pallas kernels  93.2 us (91%)
  local copies, waits for them, and re-layouts  3.33 us (3%)
  matrix products  2.72 us (3%)
  other arithmetic  2.61 us (3%)
    pallas_call x1, Pallas kernels, shards(): pl.pallas_call(kernel, out_shape=jax.ShapeDtypeStruct((FLEV, BAND, LONS),...  93.2 us
    unnamed x5, local copies, waits for them, and re-layouts  3.3 us
    dot_general x1, matrix products, shards(): jnp.einsum('kqr,krj->kqj', terms, legendre, preferred_element_type=F32)  2.72 us

profile of v2, /device:TPU:1, one launch (start us, length us, event | category | flops | bytes accessed | tf_op | source)
XLA Modules:
  0.0 101.9 jit_solution(4215831761130673891)
XLA Ops:
  0.0 0.8 dynamic-slice_subtract_fusion
  0.8 0.1 iota_compare_fusion
  1.0 0.0 copy-start.1
  1.0 1.5 %fusion.8 = (bf16[2,2,2,48,1025]{4,3,2,1,0:T(8,128)(2,1)S(1)}, bf16[2,2,2,48,1025]{4,3,2,1,0:T(8,128)(2,1)S(1)}) fusion(bf16[2,2,2,48,1025]{4,3,2,1,0:T(8,128)(2,1)} %param.3, pred[2,2,1025]{2,1,0:T(4,128)(4,1)S(1)} %pad_add_fusion), kind=kLoop, calls=%fused_computation.14 | loop fusion | flops 787200 | bytes 2365700 | tf_op jit(solution)/shard_map/neg | solution.py:327
  2.5 0.2 broadcast_select_fusion
  2.7 1.0 %copy-done.1 = bf16[2,1025,1280]{2,0,1:T(2,128)(2,1)S(1)} copy-done((bf16[2,1025,1280]{2,0,1:T(2,128)(2,1)S(1)}, bf16[2,1025,1280]{2,0,1:T(2,128)(2,1)}, u32[]{:S(2)}) %copy-start.1) | copy-done | bytes 5248024
  3.7 0.0 copy-start
  3.7 2.7 %fusion.2.sums_ref = bf16[2,384,1280]{2,1,0:T(8,128)(2,1)S(1)} fusion(bf16[2,384,1025]{2,1,0:T(8,128)(2,1)S(1)} %bitcast.2, bf16[2,1025,1280]{2,0,1:T(2,128)(2,1)S(1)} %copy-done.1), kind=kOutput, calls=%fused_computation.2 | convolution fusion | flops 2016215040 | bytes 8788480 | tf_op jit(solution)/shard_map/kqr,krj->kqj/dot_general | solution.py:335
  6.4 0.0 copy-done
  6.5 93.2 %spectral_to_grid.1 = bf16[48,80,640]{2,1,0:T(8,128)(2,1)S(1)} custom-call(s32[512]{0:T(512)S(1)} %copy-done, bf16[2,384,1280]{2,1,0:T(8,128)(2,1)S(1)} %fusion.2.sums_ref), custom_call_target="tpu_custom_call" | custom-call | tf_op jit(solution)/shard_map/spectral_to_grid/pallas_call | solution.py:338
  99.6 2.3 %copy.16 = bf16[48,80,640]{2,1,0:T(8,128)(2,1)} copy(bf16[48,80,640]{2,1,0:T(8,128)(2,1)S(1)} %spectral_to_grid.1) | data formatting | bytes 9830400
  (2 shorter events, 0.1 us)
Async XLA Ops:
  1.0 2.8 %copy-start.1 = (bf16[2,1025,1280]{2,0,1:T(2,128)(2,1)S(1)}, bf16[2,1025,1280]{2,0,1:T(2,128)(2,1)}, u32[]{:S(2)}) copy-start(bf16[2,1025,1280]{2,0,1:T(2,128)(2,1)} %param.4) | copy-start | bytes 15744004
  3.7 2.7 %copy-start = (s32[512]{0:T(512)S(1)}, s32[512]{0:T(512)}, u32[]{:S(2)}) copy-start(s32[512]{0:T(512)} %pairs_ref.1) | copy-start | bytes 6148

commit v3 on v2

--- a/solution.py
+++ b/solution.py
@@ -21,11 +21,14 @@
 PIECES = BAND // TILE
 GROUPS = FLEV // TILE
 STEPS = PIECES * GROUPS
+ROWS = 128
+CHUNKS = M // ROWS
 HALF = 4 * FLEV
 LANES = 8 * FLEV
 DEPTH = 8 * WAVES
 LAG_RELAY, LAG_FINISH, LAG_GRID = 2, 3, 4
 BASIS_FROM, BASIS_STEPS = 3, 4
+EARLY_SEND, EARLY_TURN, EARLY_GRID = 7, 12, 14
 CAUGHT_UP = 2 * (BASIS_FROM + BASIS_STEPS) - LAG_GRID
 MESH = pl.DeviceIdType.MESH
 F32 = jnp.float32
@@ -46,10 +49,26 @@
 
 
 def kernel(
-    pairs_ref, sums_ref, out_ref,
-    send, landed, whole, basis, swap_outer, swap_inner,
-    a2a_send, a2a_recv, y_send, y_recv, fwd_send, fwd_recv, core_send, core_recv,
+    pairs_hbm, spectral_hbm, legendre_hbm, out_ref,
+    pairs_smem, pairs_ref, spectral, mixed_rows, legendre, terms, sums,
+    send, early, early_in, landed, whole, basis, swap_outer, swap_inner,
+    load_sem, chunk_sem, a2a_send, a2a_recv, early_send, early_recv, y_send, y_recv, fwd_send, fwd_recv, core_send, core_recv,
 ):
+    load_pairs = pltpu.make_async_copy(pairs_hbm, pairs_smem, load_sem.at[0])
+    load_spectral = pltpu.make_async_copy(spectral_hbm, spectral, load_sem.at[1])
+    load_row = pltpu.make_async_copy(pairs_hbm, pairs_ref, load_sem.at[2])
+
+    def chunk(b, size=ROWS):
+        at = pl.ds(b * ROWS, size)
+        return pltpu.make_async_copy(legendre_hbm.at[at], mixed_rows.at[at], chunk_sem.at[b])
+
+    load_pairs.start()
+    load_spectral.start()
+    for b in range(CHUNKS):
+        chunk(b).start()
+    chunk(CHUNKS, 1).start()
+    load_row.start()
+
     wave = lax.axis_index("wave")
     field = lax.axis_index("field")
     x, z = wave // ZS, wave % ZS
@@ -73,6 +92,39 @@
 
     lax.fori_loop(1, WAVES, greet, 0)
 
+    row = iota((HALF, M + 1), 1)
+    first_member = iota((HALF, M + 1), 0) < 2 * FLEV
+    load_pairs.wait()
+    load_spectral.wait()
+    for k in range(2):
+        boundary = M - pairs_smem[(wave * FIELDS + field) * 2 + k]
+        in_first = row < boundary
+        distance = jnp.where(in_first, row, row - boundary)
+        own = jnp.where(in_first == first_member, spectral[k].astype(F32), 0.0)
+        terms[k, :HALF] = own.astype(BF16)
+        terms[k, HALF:] = jnp.where(distance % 2 == 0, own, -own).astype(BF16)
+
+    def separate(b, carry):
+        chunk(b).wait()
+        at = pl.ds(pl.multiple_of(b * ROWS, ROWS), ROWS)
+        a, c = iota((2 * ROWS, 2 * ROWS), 0), iota((2 * ROWS, 2 * ROWS), 1)
+        split = one_hot(c == a % ROWS * 2 + a // ROWS)
+        both = matmul(split, mixed_rows[at].reshape(2 * ROWS, NORTH)).astype(BF16)
+        legendre[0, at] = both[:ROWS]
+        legendre[1, at] = both[ROWS:]
+        return carry
+
+    mixed_rows[M + 1 :] = jnp.zeros((TILE - 1, 2, NORTH), BF16)
+    lax.fori_loop(0, CHUNKS, separate, 0)
+    chunk(CHUNKS, 1).wait()
+    a, c = iota((2 * TILE, 2 * TILE), 0), iota((2 * TILE, 2 * TILE), 1)
+    split = one_hot(c == a % TILE * 2 + a // TILE)
+    both = matmul(split, mixed_rows[M:].reshape(2 * TILE, NORTH)).astype(BF16)
+    for k in range(2):
+        legendre[k, M:] = both[k * TILE : (k + 1) * TILE]
+    for k in range(2):
+        sums[k] = matmul(terms[k], legendre[k, : M + 1]).astype(BF16)
+
     def turn(g):
         a, b = iota((256, 256), 0), iota((256, 256), 1)
         for south in range(2):
@@ -80,7 +132,7 @@
             for u in range(NORTH // 256):
                 start = NORTH - 256 * (u + 1) if south else 256 * u
                 rows = [
-                    sums_ref[k, lo : lo + TILE, start : start + 256]
+                    sums[k, lo : lo + TILE, start : start + 256]
                     for k in range(2)
                     for lo in range(south * HALF + g * TILE, (south + 1) * HALF, FLEV)
                 ]
@@ -91,15 +143,15 @@
                     preferred_element_type=F32,
                 )
                 at = south * NORTH // TILE + u * 16
-                send[at : at + 16, :, g * 128 : (g + 1) * 128] = turned.astype(BF16).reshape(
-                    16, TILE, 128
-                )
+                tiles = turned.astype(BF16).reshape(16, TILE, 128)
+                for i in range(16):
+                    send[(at + i) // PIECES, (at + i) % PIECES, :, g * 128 : (g + 1) * 128] = tiles[i]
 
     def scatter(p, lane, lanes, sem):
         def one(i, carry):
             peer = peer_of(i)
             pltpu.make_async_remote_copy(
-                src_ref=send.at[peer * PIECES + p, :, pl.ds(lane, lanes)],
+                src_ref=send.at[peer, p, :, pl.ds(lane, lanes)],
                 dst_ref=landed.at[p, wave, :, pl.ds(lane, lanes)],
                 send_sem=a2a_send.at[sem],
                 recv_sem=a2a_recv.at[sem],
@@ -123,11 +175,11 @@
             device_id=(wave, there), device_id_type=MESH,
         )
 
-    def to_up(t, source=field):
-        return remote(t, source, 0, y_send, y_recv, 0, up)
-
-    def to_down(t, source=field):
-        return remote(t, source, 0, y_send, y_recv, 1, down)
+    def to_up(t, part, source=field):
+        return remote(t, source, part, y_send, y_recv, part - 1, up)
+
+    def to_down(t, part, source=field):
+        return remote(t, source, part, y_send, y_recv, part + 1, down)
 
     def fwd_up(t, source=down):
         return remote(t, source, 1, fwd_send, fwd_recv, 0, up)
@@ -141,18 +193,7 @@
             source = source // 2 * 2 + other
         return remote(t, source, part, core_send, core_recv, k, mate)
 
-    def gather(t):
-        p, g = t // GROUPS, lax.rem(t, GROUPS)
-
-        @pl.when(p == 0)
-        def _():
-            wait_all(0, pl.multiple_of(g * 128, 128), 128, a2a_recv.at[g])
-
-        @pl.when(jnp.logical_and(p > 0, g == 0))
-        def _():
-            wait_all(p, 0, LANES, a2a_recv.at[GROUPS - 1 + p])
-
-        got = landed[p, :, :, pl.ds(pl.multiple_of(g * 128, 128), 128)]
+    def shuffle(t, source, got):
         got = got.reshape(2, 4, 4, TILE, 128)
         lhs = jnp.concatenate([got[:, s1].reshape(128, 128) for s1 in range(4)], axis=1)
         mixed = matmul(lhs, swap_outer[...]).astype(BF16).reshape(2, 4, TILE, 512)
@@ -173,20 +214,93 @@
         for f1 in range(4):
             for f0 in range(4):
                 for s in range(2):
-                    whole[t, field, f1 * 4 + f0, :, 128 * s : 128 * (s + 1)] = done[
+                    whole[t, source, f1 * 4 + f0, :, 128 * s : 128 * (s + 1)] = done[
                         f1, s, :, 128 * f0 : 128 * (f0 + 1)
                     ]
-        to_up(t).start()
-        to_down(t).start()
+
+    def gather(t):
+        p, g = t // GROUPS, lax.rem(t, GROUPS)
+        lane = pl.multiple_of(g * 128, 128)
+
+        @pl.when(p < 2)
+        def _():
+            wait_all(p, lane, 128, a2a_recv.at[t])
+
+        @pl.when(jnp.logical_and(p >= 2, g == 0))
+        def _():
+            wait_all(p, 0, LANES, a2a_recv.at[2 * GROUPS - 2 + p])
+
+        shuffle(t, field, landed[p, :, :, pl.ds(lane, 128)])
+        to_up(t, 1).start()
+        to_down(t, 2).start()
+        to_up(t, 2).start()
+        to_down(t, 1).start()
         to_mate(t, 0).start()
 
     def relay(t):
-        to_up(t, down).wait_recv()
+        to_up(t, 1, down).wait_recv()
         fwd_up(t).start()
+        to_down(t, 2, up).wait_recv()
+        fwd_down(t).start()
+        to_up(t, 2, down).wait_recv()
         to_mate(t, 1).start()
-        to_down(t, up).wait_recv()
-        fwd_down(t).start()
+        to_down(t, 1, up).wait_recv()
         to_mate(t, 2).start()
+
+    def along(source, lo, size, sends, recvs, slot, there):
+        block = early.at[source, pl.ds(lo, size)]
+        return pltpu.make_async_remote_copy(
+            src_ref=block, dst_ref=block, send_sem=sends.at[0, slot], recv_sem=recvs.at[0, slot],
+            device_id=(wave, there), device_id_type=MESH,
+        )
+
+    def early_up(source=y):
+        return along(source, 0, WAVES, y_send, y_recv, 0, up)
+
+    def early_down(source=y):
+        return along(source, 0, WAVES, y_send, y_recv, 1, down)
+
+    def early_fwd_up(source=down // 2):
+        return along(source, 0, WAVES // 2, fwd_send, fwd_recv, 0, up)
+
+    def early_fwd_down(source=up // 2):
+        return along(source, WAVES // 2, WAVES // 2, fwd_send, fwd_recv, 1, down)
+
+    def early_relay():
+        early_up(down // 2).wait_recv()
+        early_fwd_up().start()
+        early_down(up // 2).wait_recv()
+        early_fwd_down().start()
+
+    def early_scatter():
+        early_fwd_up(across // 2).wait_recv()
+        early_fwd_down(across // 2).wait_recv()
+        early_in[wave] = early[:, wave]
+
+        def one(i, carry):
+            peer = peer_of(i)
+            pltpu.make_async_remote_copy(
+                src_ref=early.at[:, peer],
+                dst_ref=early_in.at[wave],
+                send_sem=early_send,
+                recv_sem=early_recv,
+                device_id=(peer, field),
+                device_id_type=MESH,
+            ).start()
+            return carry
+
+        lax.fori_loop(1, WAVES, one, 0)
+
+    def early_wait(sem):
+        block = early_in.at[pl.ds(0, WAVES - 1)]
+        pltpu.make_async_copy(block, block, sem).wait()
+
+    def early_mate(source, side):
+        return remote(0, source * 2 + side, 0, core_send, core_recv, source, mate)
+
+    def early_turn(source):
+        shuffle(0, source * 2 + core, early_in[:, source])
+        early_mate(source, core).start()
 
     def finish(t):
         fwd_up(t, across).wait_recv()
@@ -197,6 +311,9 @@
     def synthesize(t):
         for k in range(5):
             to_mate(t, k, 1).wait_recv()
+        product(t)
+
+    def product(t):
         lhs = jnp.concatenate(
             [whole[t, s].reshape(TILE * TILE, DEPTH) for s in range(FIELDS)], axis=1
         )
@@ -232,34 +349,29 @@
         basis[at, :] = (weight * value).astype(BF16)
         return carry
 
-    def own(p):
-        landed[p, wave] = send[wave * PIECES + p]
-
-    def scatter_group(g):
+    load_row.wait()
+    turn(0)
+    early[y] = send[:, 0, :, :128]
+    pl.semaphore_wait(barrier, WAVES + 2)
+    early_up().start()
+    early_down().start()
+    for g in range(1, GROUPS):
         turn(g)
-        if g == 0:
-            pl.semaphore_wait(barrier, WAVES + 2)
         scatter(0, g * 128, 128, g)
-        lanes = slice(g * 128, (g + 1) * 128)
-        landed[0, wave, :, lanes] = send[wave * PIECES, :, lanes]
-
-    scatter_group(0)
-    scatter_group(1)
-
     a, b = iota((512, 512), 0), iota((512, 512), 1)
     keep = a // 16 % 8 * 16
     swap_outer[...] = one_hot(b == a // 4 % 4 * 128 + keep + a // 128 * 4 + a % 4)
     swap_inner[...] = one_hot(b == a % 4 * 128 + keep + a // 4 % 4 * 4 + a // 128)
 
-    scatter_group(2)
-    scatter(1, 0, LANES, GROUPS)
-    gather(0)
-    scatter(2, 0, LANES, GROUPS + 1)
+    early_relay()
+    scatter(1, 0, 128, GROUPS)
+    for p in range(PIECES):
+        landed[p, wave] = send[wave, p]
     gather(1)
-    relay(0)
+    scatter(1, 128, 128, GROUPS + 1)
+    scatter(1, 256, 128, GROUPS + 2)
     gather(2)
-    for p in range(1, PIECES):
-        own(p)
+    scatter(2, 0, LANES, 2 * GROUPS)
 
     def step(t, carry):
         p, g = t // GROUPS, lax.rem(t, GROUPS)
@@ -270,13 +382,13 @@
 
         @pl.when(jnp.logical_and(g == 0, p < PIECES - 2))
         def _():
-            scatter(p + 2, 0, LANES, GROUPS + 1 + p)
+            scatter(p + 2, 0, LANES, 2 * GROUPS + p)
 
         @pl.when(t < STEPS)
         def _():
             gather(t)
 
-        @pl.when(t < STEPS + LAG_FINISH)
+        @pl.when(jnp.logical_and(t > LAG_FINISH, t < STEPS + LAG_FINISH))
         def _():
             finish(t - LAG_FINISH)
 
@@ -286,9 +398,31 @@
             first = (t - BASIS_FROM) * blocks
             lax.fori_loop(first, first + blocks, basis_block, 0)
 
+        @pl.when(t == EARLY_SEND)
+        def _():
+            early_scatter()
+
+        @pl.when(t == EARLY_TURN)
+        def _():
+            early_wait(early_recv)
+
+        @pl.when(jnp.logical_and(t >= EARLY_TURN, t < EARLY_TURN + YS // 2))
+        def _():
+            early_turn(2 * (t - EARLY_TURN))
+            early_turn(2 * (t - EARLY_TURN) + 1)
+
+        @pl.when(t == EARLY_GRID)
+        def _():
+            for source in range(YS):
+                early_mate(source, other).wait_recv()
+            product(0)
+
+        @pl.when(jnp.logical_and(t > BASIS_FROM + BASIS_STEPS, t < CAUGHT_UP))
+        def _():
+            synthesize(2 * (t - BASIS_FROM - BASIS_STEPS))
+
         @pl.when(jnp.logical_and(t >= BASIS_FROM + BASIS_STEPS, t < CAUGHT_UP))
         def _():
-            synthesize(2 * (t - BASIS_FROM - BASIS_STEPS))
             synthesize(2 * (t - BASIS_FROM - BASIS_STEPS) + 1)
 
         @pl.when(t >= CAUGHT_UP)
@@ -299,64 +433,68 @@
 
     lax.fori_loop(GROUPS, STEPS + LAG_GRID, step, 0)
 
-    for g in range(GROUPS):
-        wait_all(0, g * 128, 128, a2a_send.at[g])
-    for p in range(1, PIECES):
-        wait_all(p, 0, LANES, a2a_send.at[GROUPS - 1 + p])
+    for t in range(1, 2 * GROUPS):
+        wait_all(t // GROUPS, t % GROUPS * 128, 128, a2a_send.at[t])
+    for p in range(2, PIECES):
+        wait_all(p, 0, LANES, a2a_send.at[2 * GROUPS - 2 + p])
+    early_wait(early_send)
+    early_up().wait_send()
+    early_down().wait_send()
+    early_fwd_up().wait_send()
+    early_fwd_down().wait_send()
+    for source in range(YS):
+        early_mate(source, core).wait_send()
 
     def drain(t, carry):
-        to_up(t).wait_send()
-        to_down(t).wait_send()
+        for part in (1, 2):
+            to_up(t, part).wait_send()
+            to_down(t, part).wait_send()
         fwd_up(t).wait_send()
         fwd_down(t).wait_send()
         for k in range(5):
             to_mate(t, k).wait_send()
         return carry
 
-    lax.fori_loop(0, STEPS, drain, 0)
-
-
-def hemisphere_terms(spectral, pair_ids):
-    row = jnp.arange(M + 1, dtype=jnp.int32)[None, :]
-    boundary = (M - pair_ids)[:, None]
-    in_first = row < boundary
-    odd = jnp.where(in_first, row, row - boundary) % 2 == 1
-    owner = jnp.stack([in_first, jnp.logical_not(in_first)], axis=1)[:, None, :, None, None, :]
-    flip = jnp.stack([jnp.zeros_like(odd), odd], axis=1)[:, :, None, None, None, :]
-    terms = jnp.where(owner, spectral[:, None], jnp.zeros((), BF16))
-    return jnp.where(flip, -terms, terms)
+    lax.fori_loop(1, STEPS, drain, 0)
 
 
 def shards(spectral, legendre, slot_pairs):
     per_device = spectral.shape[0]
-    start_slot = lax.axis_index(("wave", "field")) * per_device
-    own_pairs = lax.dynamic_slice_in_dim(slot_pairs, start_slot, per_device)
-    terms = hemisphere_terms(spectral, own_pairs).reshape(per_device, 2 * HALF, M + 1)
-    sums = jnp.einsum("kqr,krj->kqj", terms, legendre, preferred_element_type=F32).astype(BF16)
     dma = pltpu.SemaphoreType.DMA
     vmem = pltpu.VMEM
     return pl.pallas_call(
         kernel,
         out_shape=jax.ShapeDtypeStruct((FLEV, BAND, LONS), BF16),
-        in_specs=[pl.BlockSpec(memory_space=pltpu.VMEM)] * 2,
+        in_specs=[pl.BlockSpec(memory_space=pltpu.HBM)] * 3,
         out_specs=pl.BlockSpec(memory_space=pltpu.VMEM),
         scratch_shapes=[
-            vmem((WAVES * PIECES, TILE, LANES), BF16),
+            pltpu.SMEM((PAIRS,), jnp.int32),
+            vmem((PAIRS,), jnp.int32),
+            vmem((per_device, HALF, M + 1), BF16),
+            vmem((M + TILE, per_device, NORTH), BF16),
+            vmem((per_device, M + TILE, NORTH), BF16),
+            vmem((per_device, 2 * HALF, M + 1), BF16),
+            vmem((per_device, 2 * HALF, NORTH), BF16),
+            vmem((WAVES, PIECES, TILE, LANES), BF16),
+            vmem((YS, WAVES, TILE, 128), BF16),
+            vmem((WAVES, YS, TILE, 128), BF16),
             vmem((PIECES, WAVES, TILE, LANES), BF16),
             vmem((STEPS, FIELDS, TILE, TILE, DEPTH), BF16),
             vmem((FIELDS * DEPTH, LONS), BF16),
             vmem((512, 512), BF16),
             vmem((512, 512), BF16),
-            dma((GROUPS + PIECES - 1,)), dma((GROUPS + PIECES - 1,)),
-            dma((STEPS, 2)), dma((STEPS, 2)),
+            dma((3,)), dma((CHUNKS + 1,)),
+            dma((2 * GROUPS + PIECES - 2,)), dma((2 * GROUPS + PIECES - 2,)),
+            dma, dma,
+            dma((STEPS, 4)), dma((STEPS, 4)),
             dma((STEPS, 2)), dma((STEPS, 2)),
             dma((STEPS, 5)), dma((STEPS, 5)),
         ],
         compiler_params=pltpu.CompilerParams(
-            collective_id=0, has_side_effects=True, vmem_limit_bytes=40 << 20
+            collective_id=0, has_side_effects=True, vmem_limit_bytes=46 << 20
         ),
         name="spectral_to_grid",
-    )(slot_pairs, sums)
+    )(slot_pairs, spectral.reshape(per_device, HALF, M + 1), legendre.transpose(1, 0, 2))
 
 
 def solution(mesh):

time: 102 us -> 95.4 us (0.935)
  matrix products: 2.72 us -> 0 us
  other arithmetic: 2.61 us -> 0 us
  Pallas kernels: 93.2 us -> 91.1 us
    dot_general x1 -> x0, matrix products: 2.72 us -> none  [shards(): jnp.einsum('kqr,krj->kqj', terms, legendre, preferred_element_type=F32)]
    pallas_call x1, Pallas kernels: 93.2 us -> 91.1 us  [shards(): pl.pallas_call(kernel, out_shape=jax.ShapeDtypeStruct((FLEV, BAND, LONS),...]
    neg x1 -> x0, other arithmetic: 1.49 us -> none  [hemisphere_terms(): return jnp.where(flip, -terms, terms)]
where the time goes in v3:
time: 95.4 us; the launch traced here: 95.2 us
  Pallas kernels  91.1 us (95%)
  local copies, waits for them, and re-layouts  4.1 us (4%)
    pallas_call x1, Pallas kernels, shards(): pl.pallas_call(kernel, out_shape=jax.ShapeDtypeStruct((FLEV, BAND, LONS),...  91.1 us
    unnamed x5, local copies, waits for them, and re-layouts  4.1 us

profile of v3, /device:TPU:1, one launch (start us, length us, event | category | flops | bytes accessed | tf_op | source)
XLA Modules:
  0.0 95.2 jit_solution(9685340988176720736)
XLA Ops:
  0.0 0.0 copy-start
  0.0 1.2 %copy-done = bf16[2,2,2,48,1025]{4,3,2,1,0:T(8,128)(2,1)S(1)} copy-done((bf16[2,2,2,48,1025]{4,3,2,1,0:T(8,128)(2,1)S(1)}, bf16[2,2,2,48,1025]{4,3,2,1,0:T(8,128)(2,1)}, u32[]{:S(2)}) %copy-start) | copy-done | bytes 787224
  1.2 0.0 copy-start.1
  1.2 0.7 copy-done.1
  1.9 91.1 %spectral_to_grid.1 = bf16[48,80,640]{2,1,0:T(8,128)(2,1)S(1)} custom-call(s32[512]{0:T(512)S(1)} %copy-done.1, bf16[2,192,1025]{2,1,0:T(8,128)(2,1)S(1)} %bitcast.2, bf16[1025,2,1280]{2,1,0:T(2,128)(2,1)} %bitcast.3), custom_call_target="tpu_custom_call" | custom-call | tf_op jit(solution)/shard_map/spectral_to_grid/pallas_call | solution.py:465
  93.0 2.3 %copy.5 = bf16[48,80,640]{2,1,0:T(8,128)(2,1)} copy(bf16[48,80,640]{2,1,0:T(8,128)(2,1)S(1)} %spectral_to_grid.1) | data formatting | bytes 9830400
Async XLA Ops:
  0.0 1.2 %copy-start = (bf16[2,2,2,48,1025]{4,3,2,1,0:T(8,128)(2,1)S(1)}, bf16[2,2,2,48,1025]{4,3,2,1,0:T(8,128)(2,1)}, u32[]{:S(2)}) copy-start(bf16[2,2,2,48,1025]{4,3,2,1,0:T(8,128)(2,1)} %param.3) | copy-start | bytes 2361604
  1.2 0.7 copy-start.1

commit v4 on v3

--- a/solution.py
+++ b/solution.py
@@ -26,7 +26,7 @@
 HALF = 4 * FLEV
 LANES = 8 * FLEV
 DEPTH = 8 * WAVES
-LAG_RELAY, LAG_FINISH, LAG_GRID = 2, 3, 4
+LAG_RELAY, LAG_GRID = 2, 4
 BASIS_FROM, BASIS_STEPS = 3, 4
 EARLY_SEND, EARLY_TURN, EARLY_GRID = 7, 12, 14
 CAUGHT_UP = 2 * (BASIS_FROM + BASIS_STEPS) - LAG_GRID
@@ -51,7 +51,7 @@
 def kernel(
     pairs_hbm, spectral_hbm, legendre_hbm, out_ref,
     pairs_smem, pairs_ref, spectral, mixed_rows, legendre, terms, sums,
-    send, early, early_in, landed, whole, basis, swap_outer, swap_inner,
+    send, early, early_in, landed, whole, basis, swap_outer, swap_inner, kept, partial, outgoing, incoming,
     load_sem, chunk_sem, a2a_send, a2a_recv, early_send, early_recv, y_send, y_recv, fwd_send, fwd_recv, core_send, core_recv,
 ):
     load_pairs = pltpu.make_async_copy(pairs_hbm, pairs_smem, load_sem.at[0])
@@ -73,11 +73,8 @@
     field = lax.axis_index("field")
     x, z = wave // ZS, wave % ZS
     y, core = field // 2, field % 2
-    up = lax.rem(y + 1, YS) * 2 + core
-    down = lax.rem(y + YS - 1, YS) * 2 + core
-    across = lax.rem(y + 2, YS) * 2 + core
-    other = 1 - core
-    mate = y * 2 + other
+    above, below, across = lax.rem(y + 1, YS), lax.rem(y + YS - 1, YS), lax.rem(y + 2, YS)
+    up, down, mate = above * 2 + core, below * 2 + core, y * 2 + 1 - core
 
     def peer_of(i):
         return lax.rem(x + i // ZS, XS) * ZS + lax.rem(z + i % ZS, ZS)
@@ -101,8 +98,14 @@
         in_first = row < boundary
         distance = jnp.where(in_first, row, row - boundary)
         own = jnp.where(in_first == first_member, spectral[k].astype(F32), 0.0)
-        terms[k, :HALF] = own.astype(BF16)
-        terms[k, HALF:] = jnp.where(distance % 2 == 0, own, -own).astype(BF16)
+        mirrored = jnp.where(distance % 2 == 0, own, -own).astype(BF16)
+        own = own.astype(BF16)
+        for g in range(GROUPS):
+            for part in range(4):
+                rows = slice(part * FLEV + g * TILE, part * FLEV + (g + 1) * TILE)
+                at = g * 128 + part * TILE
+                terms[k, at : at + TILE] = own[rows]
+                terms[k, at + 64 : at + 64 + TILE] = mirrored[rows]
 
     def separate(b, carry):
         chunk(b).wait()
@@ -122,8 +125,11 @@
     both = matmul(split, mixed_rows[M:].reshape(2 * TILE, NORTH)).astype(BF16)
     for k in range(2):
         legendre[k, M:] = both[k * TILE : (k + 1) * TILE]
-    for k in range(2):
-        sums[k] = matmul(terms[k], legendre[k, : M + 1]).astype(BF16)
+
+    def group_sums(g):
+        rows = slice(g * 128, (g + 1) * 128)
+        for k in range(2):
+            sums[k, rows] = matmul(terms[k, rows], legendre[k, : M + 1]).astype(BF16)
 
     def turn(g):
         a, b = iota((256, 256), 0), iota((256, 256), 1)
@@ -134,7 +140,7 @@
                 rows = [
                     sums[k, lo : lo + TILE, start : start + 256]
                     for k in range(2)
-                    for lo in range(south * HALF + g * TILE, (south + 1) * HALF, FLEV)
+                    for lo in range(g * 128 + south * 64, g * 128 + south * 64 + 64, TILE)
                 ]
                 turned = lax.dot_general(
                     pick,
@@ -175,23 +181,24 @@
             device_id=(wave, there), device_id_type=MESH,
         )
 
-    def to_up(t, part, source=field):
+    def to_up(t, part, source=y):
         return remote(t, source, part, y_send, y_recv, part - 1, up)
 
-    def to_down(t, part, source=field):
+    def to_down(t, part, source=y):
         return remote(t, source, part, y_send, y_recv, part + 1, down)
 
-    def fwd_up(t, source=down):
+    def fwd_up(t, source=below):
         return remote(t, source, 1, fwd_send, fwd_recv, 0, up)
 
-    def fwd_down(t, source=up):
+    def fwd_down(t, source=above):
         return remote(t, source, 2, fwd_send, fwd_recv, 1, down)
 
-    def to_mate(t, k, flip=0):
-        source, part = ((field, 0), (down, 0), (up, 0), (across, 1), (across, 2))[k]
-        if flip:
-            source = source // 2 * 2 + other
-        return remote(t, source, part, core_send, core_recv, k, mate)
+    def to_mate(t):
+        return pltpu.make_async_remote_copy(
+            src_ref=outgoing.at[t], dst_ref=incoming.at[t],
+            send_sem=core_send.at[t], recv_sem=core_recv.at[t],
+            device_id=(wave, mate), device_id_type=MESH,
+        )
 
     def shuffle(t, source, got):
         got = got.reshape(2, 4, 4, TILE, 128)
@@ -230,22 +237,17 @@
         def _():
             wait_all(p, 0, LANES, a2a_recv.at[2 * GROUPS - 2 + p])
 
-        shuffle(t, field, landed[p, :, :, pl.ds(lane, 128)])
+        shuffle(t, y, landed[p, :, :, pl.ds(lane, 128)])
         to_up(t, 1).start()
         to_down(t, 2).start()
         to_up(t, 2).start()
         to_down(t, 1).start()
-        to_mate(t, 0).start()
 
     def relay(t):
-        to_up(t, 1, down).wait_recv()
+        to_up(t, 1, below).wait_recv()
         fwd_up(t).start()
-        to_down(t, 2, up).wait_recv()
+        to_down(t, 2, above).wait_recv()
         fwd_down(t).start()
-        to_up(t, 2, down).wait_recv()
-        to_mate(t, 1).start()
-        to_down(t, 1, up).wait_recv()
-        to_mate(t, 2).start()
 
     def along(source, lo, size, sends, recvs, slot, there):
         block = early.at[source, pl.ds(lo, size)]
@@ -260,21 +262,21 @@
     def early_down(source=y):
         return along(source, 0, WAVES, y_send, y_recv, 1, down)
 
-    def early_fwd_up(source=down // 2):
+    def early_fwd_up(source=below):
         return along(source, 0, WAVES // 2, fwd_send, fwd_recv, 0, up)
 
-    def early_fwd_down(source=up // 2):
+    def early_fwd_down(source=above):
         return along(source, WAVES // 2, WAVES // 2, fwd_send, fwd_recv, 1, down)
 
     def early_relay():
-        early_up(down // 2).wait_recv()
+        early_up(below).wait_recv()
         early_fwd_up().start()
-        early_down(up // 2).wait_recv()
+        early_down(above).wait_recv()
         early_fwd_down().start()
 
     def early_scatter():
-        early_fwd_up(across // 2).wait_recv()
-        early_fwd_down(across // 2).wait_recv()
+        early_fwd_up(across).wait_recv()
+        early_fwd_down(across).wait_recv()
         early_in[wave] = early[:, wave]
 
         def one(i, carry):
@@ -295,32 +297,31 @@
         block = early_in.at[pl.ds(0, WAVES - 1)]
         pltpu.make_async_copy(block, block, sem).wait()
 
-    def early_mate(source, side):
-        return remote(0, source * 2 + side, 0, core_send, core_recv, source, mate)
-
-    def early_turn(source):
-        shuffle(0, source * 2 + core, early_in[:, source])
-        early_mate(source, core).start()
-
-    def finish(t):
+    def split(t, slot, values):
+        outgoing[t] = values[:, LONS:].astype(BF16).reshape(TILE, TILE, LONS)
+        to_mate(t).start()
+        kept[slot] = values[:, :LONS]
+
+    def columns(t, source):
+        return whole[t, source].reshape(TILE * TILE, DEPTH)
+
+    def product(t, slot):
+        lhs = jnp.concatenate([columns(t, s) for s in range(YS)], axis=1)
+        split(t, slot, matmul(lhs, basis[...]))
+
+    def synthesize(t):
+        to_up(t, 2, below).wait_recv()
+        to_down(t, 1, above).wait_recv()
         fwd_up(t, across).wait_recv()
-        to_mate(t, 3).start()
         fwd_down(t, across).wait_recv()
-        to_mate(t, 4).start()
-
-    def synthesize(t):
-        for k in range(5):
-            to_mate(t, k, 1).wait_recv()
-        product(t)
-
-    def product(t):
-        lhs = jnp.concatenate(
-            [whole[t, s].reshape(TILE * TILE, DEPTH) for s in range(FIELDS)], axis=1
-        )
-        values = matmul(lhs, basis[...]).astype(BF16).reshape(TILE, TILE, LONS)
+        product(t, lax.rem(t, 2))
+
+    def combine(t, slot):
+        to_mate(t).wait_recv()
+        values = kept[slot] + incoming[t].reshape(TILE * TILE, LONS).astype(F32)
         levels = pl.ds(pl.multiple_of(lax.rem(t, GROUPS) * TILE, TILE), TILE)
         lats = pl.ds(pl.multiple_of(t // GROUPS * TILE, TILE), TILE)
-        out_ref[levels, lats, :] = values
+        out_ref[levels, lats, :] = values.astype(BF16).reshape(TILE, TILE, LONS)
 
     size = 128
 
@@ -329,7 +330,7 @@
         r = i * size + iota((size, 1), 0)
         inside = r % DEPTH
         source = inside // 128 * 16 + inside % 16
-        slot = (source * FIELDS + r // DEPTH) * 2 + inside // 64 % 2
+        slot = (source * FIELDS + r // DEPTH * 2 + core) * 2 + inside // 64 % 2
         pairs = jnp.broadcast_to(pairs_ref[...].reshape(1, PAIRS), (size, PAIRS))
         pair = jnp.sum(
             jnp.where(iota((size, PAIRS), 1) == slot, pairs, 0).astype(F32), axis=1, keepdims=True
@@ -337,7 +338,9 @@
         number = jnp.where(r // 32 % 2 == 0, pair, M - 1.0 - pair)
         part = (r // 16 % 2).astype(F32)
         weight = jnp.where(number == 0.0, 1.0 / math.sqrt(2.0 * M), 2.0 / math.sqrt(2.0 * M))
-        longitude = (field * LONS + iota((size, LONS), 1)).astype(F32)
+        column = iota((size, 2 * LONS), 1)
+        longitude = jnp.where(column < LONS, field * LONS + column, (mate - 1) * LONS + column)
+        longitude = longitude.astype(F32)
         phase = number * longitude + part * (NLON // 4)
         phase = phase - NLON * jnp.floor(phase * (1.0 / NLON) + 0.5)
         turns = 0.25 - jnp.abs(phase) * (1.0 / NLON)
@@ -350,14 +353,18 @@
         return carry
 
     load_row.wait()
+    group_sums(1)
+    turn(1)
+    pl.semaphore_wait(barrier, WAVES + 2)
+    scatter(0, 128, 128, 1)
+    group_sums(0)
     turn(0)
     early[y] = send[:, 0, :, :128]
-    pl.semaphore_wait(barrier, WAVES + 2)
     early_up().start()
     early_down().start()
-    for g in range(1, GROUPS):
-        turn(g)
-        scatter(0, g * 128, 128, g)
+    group_sums(2)
+    turn(2)
+    scatter(0, 256, 128, 2)
     a, b = iota((512, 512), 0), iota((512, 512), 1)
     keep = a // 16 % 8 * 16
     swap_outer[...] = one_hot(b == a // 4 % 4 * 128 + keep + a // 128 * 4 + a % 4)
@@ -388,13 +395,9 @@
         def _():
             gather(t)
 
-        @pl.when(jnp.logical_and(t > LAG_FINISH, t < STEPS + LAG_FINISH))
-        def _():
-            finish(t - LAG_FINISH)
-
         @pl.when(t < BASIS_FROM + BASIS_STEPS)
         def _():
-            blocks = FIELDS * DEPTH // size // BASIS_STEPS
+            blocks = YS * DEPTH // size // BASIS_STEPS
             first = (t - BASIS_FROM) * blocks
             lax.fori_loop(first, first + blocks, basis_block, 0)
 
@@ -408,30 +411,53 @@
 
         @pl.when(jnp.logical_and(t >= EARLY_TURN, t < EARLY_TURN + YS // 2))
         def _():
-            early_turn(2 * (t - EARLY_TURN))
-            early_turn(2 * (t - EARLY_TURN) + 1)
+            for i in range(2):
+                source = 2 * (t - EARLY_TURN) + i
+                shuffle(0, source, early_in[:, source])
 
         @pl.when(t == EARLY_GRID)
         def _():
-            for source in range(YS):
-                early_mate(source, other).wait_recv()
-            product(0)
+            product(0, 2)
 
         @pl.when(jnp.logical_and(t > BASIS_FROM + BASIS_STEPS, t < CAUGHT_UP))
         def _():
-            synthesize(2 * (t - BASIS_FROM - BASIS_STEPS))
-
-        @pl.when(jnp.logical_and(t >= BASIS_FROM + BASIS_STEPS, t < CAUGHT_UP))
-        def _():
-            synthesize(2 * (t - BASIS_FROM - BASIS_STEPS) + 1)
-
-        @pl.when(t >= CAUGHT_UP)
-        def _():
-            synthesize(t - LAG_GRID)
+            n = 2 * (t - BASIS_FROM - BASIS_STEPS)
+            synthesize(n)
+            combine(n - 1, 1)
+
+        @pl.when(t >= BASIS_FROM + BASIS_STEPS)
+        def _():
+            n = jnp.where(t < CAUGHT_UP, 2 * (t - BASIS_FROM - BASIS_STEPS) + 1, t - LAG_GRID)
+            synthesize(n)
+
+            @pl.when(n > 1)
+            def _():
+                combine(n - 1, lax.rem(n - 1, 2))
 
         return carry
 
-    lax.fori_loop(GROUPS, STEPS + LAG_GRID, step, 0)
+    lax.fori_loop(GROUPS, STEPS + LAG_RELAY, step, 0)
+
+    last = STEPS - 1
+
+    def last_sum(sources):
+        rows = [pl.ds(pl.multiple_of(s * DEPTH, DEPTH), DEPTH) for s in sources]
+        return matmul(
+            jnp.concatenate([columns(last, s) for s in sources], axis=1),
+            jnp.concatenate([basis[at, :] for at in rows], axis=0),
+        )
+
+    synthesize(last - 1)
+    combine(last - 2, last % 2)
+    to_up(last, 2, below).wait_recv()
+    to_down(last, 1, above).wait_recv()
+    partial[...] = last_sum([y, below, above])
+    fwd_up(last, across).wait_recv()
+    fwd_down(last, across).wait_recv()
+    split(last, last % 2, partial[...] + last_sum([across]))
+    combine(last - 1, (last - 1) % 2)
+    combine(0, 2)
+    combine(last, last % 2)
 
     for t in range(1, 2 * GROUPS):
         wait_all(t // GROUPS, t % GROUPS * 128, 128, a2a_send.at[t])
@@ -442,8 +468,7 @@
     early_down().wait_send()
     early_fwd_up().wait_send()
     early_fwd_down().wait_send()
-    for source in range(YS):
-        early_mate(source, core).wait_send()
+    to_mate(0).wait_send()
 
     def drain(t, carry):
         for part in (1, 2):
@@ -451,8 +476,7 @@
             to_down(t, part).wait_send()
         fwd_up(t).wait_send()
         fwd_down(t).wait_send()
-        for k in range(5):
-            to_mate(t, k).wait_send()
+        to_mate(t).wait_send()
         return carry
 
     lax.fori_loop(1, STEPS, drain, 0)
@@ -464,7 +488,7 @@
     vmem = pltpu.VMEM
     return pl.pallas_call(
         kernel,
-        out_shape=jax.ShapeDtypeStruct((FLEV, BAND, LONS), BF16),
+        out_shape=vmem((FLEV, BAND, LONS), BF16),
         in_specs=[pl.BlockSpec(memory_space=pltpu.HBM)] * 3,
         out_specs=pl.BlockSpec(memory_space=pltpu.VMEM),
         scratch_shapes=[
@@ -479,22 +503,30 @@
             vmem((YS, WAVES, TILE, 128), BF16),
             vmem((WAVES, YS, TILE, 128), BF16),
             vmem((PIECES, WAVES, TILE, LANES), BF16),
-            vmem((STEPS, FIELDS, TILE, TILE, DEPTH), BF16),
-            vmem((FIELDS * DEPTH, LONS), BF16),
+            vmem((STEPS, YS, TILE, TILE, DEPTH), BF16),
+            vmem((YS * DEPTH, 2 * LONS), BF16),
             vmem((512, 512), BF16),
             vmem((512, 512), BF16),
+            vmem((3, TILE * TILE, LONS), F32),
+            vmem((TILE * TILE, 2 * LONS), F32),
+            vmem((STEPS, TILE, TILE, LONS), BF16),
+            vmem((STEPS, TILE, TILE, LONS), BF16),
             dma((3,)), dma((CHUNKS + 1,)),
             dma((2 * GROUPS + PIECES - 2,)), dma((2 * GROUPS + PIECES - 2,)),
             dma, dma,
             dma((STEPS, 4)), dma((STEPS, 4)),
             dma((STEPS, 2)), dma((STEPS, 2)),
-            dma((STEPS, 5)), dma((STEPS, 5)),
+            dma((STEPS,)), dma((STEPS,)),
         ],
         compiler_params=pltpu.CompilerParams(
-            collective_id=0, has_side_effects=True, vmem_limit_bytes=46 << 20
+            collective_id=0, has_side_effects=True, vmem_limit_bytes=50 << 20
         ),
         name="spectral_to_grid",
-    )(slot_pairs, spectral.reshape(per_device, HALF, M + 1), legendre.transpose(1, 0, 2))
+    )(
+        pltpu.with_memory_space_constraint(slot_pairs, pltpu.HBM),
+        pltpu.with_memory_space_constraint(spectral.reshape(per_device, HALF, M + 1), pltpu.HBM),
+        pltpu.with_memory_space_constraint(legendre.transpose(1, 0, 2), pltpu.HBM),
+    )
 
 
 def solution(mesh):

time: 95.4 us -> 92.4 us (0.969)
  local copies, waits for them, and re-layouts: 4.1 us -> 2.25 us
  Pallas kernels: 91.1 us -> 90.1 us
    unnamed x5 -> x1, local copies, waits for them, and re-layouts: 4.1 us -> 2.25 us
    pallas_call x1, Pallas kernels: 91.1 us -> 90.1 us  [shards(): pl.pallas_call(kernel, out_shape=vmem((FLEV, BAND, LONS), BF16), in_specs...]
where the time goes in v4:
time: 92.4 us; the launch traced here: 92.3 us
  Pallas kernels  90.1 us (98%)
  local copies, waits for them, and re-layouts  2.25 us (2%)
    pallas_call x1, Pallas kernels, shards(): pl.pallas_call(kernel, out_shape=vmem((FLEV, BAND, LONS), BF16), in_specs...  90.1 us
    unnamed x1, local copies, waits for them, and re-layouts  2.25 us

profile of v4, /device:TPU:1, one launch (start us, length us, event | category | flops | bytes accessed | tf_op | source)
XLA Modules:
  0.0 92.3 jit_solution(16611178477727846687)
XLA Ops:
  0.0 90.1 %spectral_to_grid.1 = bf16[48,80,640]{2,1,0:T(8,128)(2,1)S(1)} custom-call(s32[512]{0:T(512)} %pairs_hbm.1, bf16[2,192,1025]{2,1,0:T(8,128)(2,1)} %bitcast.3, bf16[1025,2,1280]{2,1,0:T(2,128)(2,1)} %bitcast.2), custom_call_target="tpu_custom_call" | custom-call | tf_op jit(solution)/shard_map/spectral_to_grid/pallas_call | solution.py:489
  90.1 2.3 %copy.5 = bf16[48,80,640]{2,1,0:T(8,128)(2,1)} copy(bf16[48,80,640]{2,1,0:T(8,128)(2,1)S(1)} %spectral_to_grid.1) | data formatting | bytes 9830400

commit v5 on v4

--- a/solution.py
+++ b/solution.py
@@ -28,7 +28,7 @@
 DEPTH = 8 * WAVES
 LAG_RELAY, LAG_GRID = 2, 4
 BASIS_FROM, BASIS_STEPS = 3, 4
-EARLY_SEND, EARLY_TURN, EARLY_GRID = 7, 12, 14
+EARLY_SEND, EARLY_TURN, EARLY_GRID = 8, 13, 15
 CAUGHT_UP = 2 * (BASIS_FROM + BASIS_STEPS) - LAG_GRID
 MESH = pl.DeviceIdType.MESH
 F32 = jnp.float32
@@ -89,36 +89,39 @@
 
     lax.fori_loop(1, WAVES, greet, 0)
 
-    row = iota((HALF, M + 1), 1)
-    first_member = iota((HALF, M + 1), 0) < 2 * FLEV
+    a, c = iota((2 * ROWS, 2 * ROWS), 0), iota((2 * ROWS, 2 * ROWS), 1)
+    swap_outer[: 2 * ROWS, : 2 * ROWS] = one_hot(c == a % ROWS * 2 + a // ROWS)
+    mixed_rows[M + 1 :] = jnp.zeros((TILE - 1, 2, NORTH), BF16)
+
+    row = iota((TILE, M + 1), 1)
     load_pairs.wait()
     load_spectral.wait()
     for k in range(2):
         boundary = M - pairs_smem[(wave * FIELDS + field) * 2 + k]
         in_first = row < boundary
-        distance = jnp.where(in_first, row, row - boundary)
-        own = jnp.where(in_first == first_member, spectral[k].astype(F32), 0.0)
-        mirrored = jnp.where(distance % 2 == 0, own, -own).astype(BF16)
-        own = own.astype(BF16)
-        for g in range(GROUPS):
-            for part in range(4):
-                rows = slice(part * FLEV + g * TILE, part * FLEV + (g + 1) * TILE)
+        odd = jnp.where(in_first, row, row - boundary) % 2 == 1
+        owners = [one_hot(in_first), one_hot(jnp.logical_not(in_first))]
+        sign = jnp.where(odd, -1.0, 1.0).astype(BF16)
+        for part in range(4):
+            for g in range(GROUPS):
                 at = g * 128 + part * TILE
-                terms[k, at : at + TILE] = own[rows]
-                terms[k, at + 64 : at + 64 + TILE] = mirrored[rows]
-
-    def separate(b, carry):
-        chunk(b).wait()
-        at = pl.ds(pl.multiple_of(b * ROWS, ROWS), ROWS)
-        a, c = iota((2 * ROWS, 2 * ROWS), 0), iota((2 * ROWS, 2 * ROWS), 1)
-        split = one_hot(c == a % ROWS * 2 + a // ROWS)
-        both = matmul(split, mixed_rows[at].reshape(2 * ROWS, NORTH)).astype(BF16)
-        legendre[0, at] = both[:ROWS]
-        legendre[1, at] = both[ROWS:]
+                lo = part * FLEV + g * TILE
+                own = spectral[k, lo : lo + TILE] * owners[part // 2]
+                terms[k, at : at + TILE] = own
+                terms[k, at + 64 : at + 64 + TILE] = own * sign
+
+    def separate(i, carry):
+        for n in range(2):
+            b = 2 * i + n
+            chunk(b).wait()
+            at = pl.ds(pl.multiple_of(b * ROWS, ROWS), ROWS)
+            rows = mixed_rows[at].reshape(2 * ROWS, NORTH)
+            both = matmul(swap_outer[: 2 * ROWS, : 2 * ROWS], rows).astype(BF16)
+            legendre[0, at] = both[:ROWS]
+            legendre[1, at] = both[ROWS:]
         return carry
 
-    mixed_rows[M + 1 :] = jnp.zeros((TILE - 1, 2, NORTH), BF16)
-    lax.fori_loop(0, CHUNKS, separate, 0)
+    lax.fori_loop(0, CHUNKS // 2, separate, 0)
     chunk(CHUNKS, 1).wait()
     a, c = iota((2 * TILE, 2 * TILE), 0), iota((2 * TILE, 2 * TILE), 1)
     split = one_hot(c == a % TILE * 2 + a // TILE)
@@ -200,6 +203,14 @@
             device_id=(wave, mate), device_id_type=MESH,
         )
 
+    def half_to_mate(half):
+        block = pl.ds(half * TILE // 2, TILE // 2)
+        return pltpu.make_async_remote_copy(
+            src_ref=outgoing.at[STEPS - 1, block], dst_ref=incoming.at[STEPS - 1, block],
+            send_sem=core_send.at[STEPS - 1 + half], recv_sem=core_recv.at[STEPS - 1 + half],
+            device_id=(wave, mate), device_id_type=MESH,
+        )
+
     def shuffle(t, source, got):
         got = got.reshape(2, 4, 4, TILE, 128)
         lhs = jnp.concatenate([got[:, s1].reshape(128, 128) for s1 in range(4)], axis=1)
@@ -318,6 +329,9 @@
 
     def combine(t, slot):
         to_mate(t).wait_recv()
+        settle(t, slot)
+
+    def settle(t, slot):
         values = kept[slot] + incoming[t].reshape(TILE * TILE, LONS).astype(F32)
         levels = pl.ds(pl.multiple_of(lax.rem(t, GROUPS) * TILE, TILE), TILE)
         lats = pl.ds(pl.multiple_of(t // GROUPS * TILE, TILE), TILE)
@@ -452,12 +466,21 @@
     to_up(last, 2, below).wait_recv()
     to_down(last, 1, above).wait_recv()
     partial[...] = last_sum([y, below, above])
-    fwd_up(last, across).wait_recv()
-    fwd_down(last, across).wait_recv()
-    split(last, last % 2, partial[...] + last_sum([across]))
+    rows = TILE * TILE // 2
+    block = basis[pl.ds(pl.multiple_of(across * DEPTH, DEPTH), DEPTH), :]
+    for half, arrival in enumerate((fwd_up(last, across), fwd_down(last, across))):
+        arrival.wait_recv()
+        levels = slice(half * TILE // 2, (half + 1) * TILE // 2)
+        at = slice(half * rows, (half + 1) * rows)
+        values = partial[at] + matmul(whole[last, across, levels].reshape(rows, DEPTH), block)
+        outgoing[last, levels] = values[:, LONS:].astype(BF16).reshape(TILE // 2, TILE, LONS)
+        half_to_mate(half).start()
+        kept[last % 2, at] = values[:, :LONS]
     combine(last - 1, (last - 1) % 2)
     combine(0, 2)
-    combine(last, last % 2)
+    half_to_mate(0).wait_recv()
+    half_to_mate(1).wait_recv()
+    settle(last, last % 2)
 
     for t in range(1, 2 * GROUPS):
         wait_all(t // GROUPS, t % GROUPS * 128, 128, a2a_send.at[t])
@@ -468,7 +491,6 @@
     early_down().wait_send()
     early_fwd_up().wait_send()
     early_fwd_down().wait_send()
-    to_mate(0).wait_send()
 
     def drain(t, carry):
         for part in (1, 2):
@@ -476,10 +498,13 @@
             to_down(t, part).wait_send()
         fwd_up(t).wait_send()
         fwd_down(t).wait_send()
+        return carry
+
+    lax.fori_loop(1, STEPS, drain, 0)
+    for t in range(STEPS - 1):
         to_mate(t).wait_send()
-        return carry
-
-    lax.fori_loop(1, STEPS, drain, 0)
+    for half in range(2):
+        half_to_mate(half).wait_send()
 
 
 def shards(spectral, legendre, slot_pairs):
@@ -516,7 +541,7 @@
             dma, dma,
             dma((STEPS, 4)), dma((STEPS, 4)),
             dma((STEPS, 2)), dma((STEPS, 2)),
-            dma((STEPS,)), dma((STEPS,)),
+            dma((STEPS + 1,)), dma((STEPS + 1,)),
         ],
         compiler_params=pltpu.CompilerParams(
             collective_id=0, has_side_effects=True, vmem_limit_bytes=50 << 20

time: 92.4 us -> 92 us (level)
  no operation moved by 1% of the time
where the time goes in v5:
time: 92 us; the launch traced here: 91.9 us
  Pallas kernels  89.7 us (98%)
  local copies, waits for them, and re-layouts  2.25 us (2%)
    pallas_call x1, Pallas kernels, shards(): pl.pallas_call(kernel, out_shape=vmem((FLEV, BAND, LONS), BF16), in_specs...  89.7 us
    unnamed x1, local copies, waits for them, and re-layouts  2.25 us

profile of v5, /device:TPU:1, one launch (start us, length us, event | category | flops | bytes accessed | tf_op | source)
XLA Modules:
  0.0 91.9 jit_solution(15294725796742680631)
XLA Ops:
  0.0 89.7 %spectral_to_grid.1 = bf16[48,80,640]{2,1,0:T(8,128)(2,1)S(1)} custom-call(s32[512]{0:T(512)} %pairs_hbm.1, bf16[2,192,1025]{2,1,0:T(8,128)(2,1)} %bitcast.3, bf16[1025,2,1280]{2,1,0:T(2,128)(2,1)} %bitcast.2), custom_call_target="tpu_custom_call" | custom-call | tf_op jit(solution)/shard_map/spectral_to_grid/pallas_call | solution.py:514
  89.7 2.3 %copy.5 = bf16[48,80,640]{2,1,0:T(8,128)(2,1)} copy(bf16[48,80,640]{2,1,0:T(8,128)(2,1)S(1)} %spectral_to_grid.1) | data formatting | bytes 9830400
